TPU v7x, 32 devices: a whole 2x2x4 slice. The times are simulated.
32 devices in a mesh: lon: 8 (over z, x), lat: 4 (over y, core).
Axes of the slice: x: 2, y: 2, z: 4, core: 2. Of those that a mesh axis runs over, the one named last changes fastest.
Arguments:
- piece_height: float32 [64, 128, 128], P('lon', 'lat')
- piece_weight: float32 [64, 128, 128], P('lon', 'lat'), may hold values from 0.05 to 2
- piece_column: int32 [64], P('lon'), may hold values from 0 to 32640, as said below
- piece_width: int32 [64], P('lon'), may hold values from 64 to 128
Outputs:
- solution_field: float32 [128, 32768], P('lat', 'lon')
- residual: float32 [128, 32768], P('lat', 'lon')
Inputs may be any that keep to these rules, and one draw needn't show every extreme that they name: Every value is a multiple of 128 and a piece lies inside one tile of 4096 columns, tile piece_column // 4096. The pieces of one device name each tile at most 2 times; one tile is named exactly 2 times by the pieces of every device.
All inputs are finite; a program needn't handle non-finite values.
Results may differ from a plain program's by a relative error of at most 0.0007.
Values sent between devices are 32-bit elements; how exact they have to be, the bound alone decides.
A program may use at most 128 MiB of HBM per device.

v0:
```python
import jax
import jax.numpy as jnp
from jax import lax
from jax.sharding import PartitionSpec as P

ROWS = 128
COLS_DEV = 4096
CAPACITY = 2
ITERS = 4


MU_DATA = 0.5
DAMPING = 0.5
RIDGE = 0.05
HIGHEST = lax.Precision.HIGHEST


def padded_2(block, sides, width):
    for axis, dim in sides:
        count = lax.axis_size(axis)
        forward = [(i, i + 1) for i in range(count - 1)]
        forward.append((count - 1, 0))
        backward = [(target, source) for source, target in forward]
        low = lax.ppermute(
            lax.slice_in_dim(block, block.shape[dim] - width, None, axis=dim), axis, forward
        )
        high = lax.ppermute(lax.slice_in_dim(block, 0, width, axis=dim), axis, backward)
        block = jnp.concatenate([low, block, high], axis=dim)
    return block


def passed_along(block, axis, distance):
    devices = range(lax.axis_size(axis))
    route = [(i - distance, i) for i in devices if i - distance in devices]
    return lax.ppermute(block, axis, route)


def piece_terms(height, weight, width, north_step, row_global):
    column = jnp.arange(height.shape[2], dtype=jnp.int32)
    valid_cell = column[None, None, :] < width[:, None, None]
    east_edge = column[None, None, :] + 1 < width[:, None, None]
    north_edge = valid_cell & (row_global[None, :, None] < ROWS - 1)
    east_step = jnp.concatenate(
        [height[:, :, 1:] - height[:, :, :-1], jnp.zeros_like(height[:, :, :1])], axis=2
    )
    cell_weight = jnp.where(valid_cell, weight, jnp.float32(0.0))
    east_weight = jnp.where(east_edge, weight, jnp.float32(0.0))
    north_weight = jnp.where(north_edge, weight, jnp.float32(0.0))
    return (
        cell_weight,
        cell_weight * height,
        east_weight,
        east_weight * east_step,
        north_weight,
        north_weight * north_step,
    )


def north_steps(height, next_first):
    inner = height[:, 1:, :] - height[:, :-1, :]
    return jnp.concatenate([inner, next_first - height[:, -1:, :]], axis=1)


def operate(field, diagonal, has_upper, has_lower):
    padded = padded_2(field, (("lon", 1), ("lat", 0)), 1)
    coupling = 2.0 * field - padded[1:-1, :-2] - padded[1:-1, 2:]
    coupling = coupling + jnp.where(has_upper, field - padded[2:, 1:-1], jnp.float32(0.0))
    coupling = coupling + jnp.where(has_lower, field - padded[:-2, 1:-1], jnp.float32(0.0))
    return diagonal * field + coupling


def squares(residual):
    return lax.psum(jnp.sum(residual * residual), ("lon", "lat"))


def body(piece_height, piece_weight, piece_column, piece_width):
    pieces, rows_dev, block_width = piece_height.shape
    lon_count = lax.axis_size("lon")
    slot_count = lon_count * CAPACITY
    tile_blocks = COLS_DEV // block_width
    flat_size = rows_dev * block_width
    row_global = lax.axis_index("lat") * rows_dev + jnp.arange(rows_dev, dtype=jnp.int32)
    target_tile = piece_column // COLS_DEV
    tile_block = piece_column % COLS_DEV // block_width
    order_ids = jnp.arange(pieces, dtype=jnp.int32)
    same_tile = target_tile[:, None] == target_tile[None, :]
    earlier = order_ids[None, :] < order_ids[:, None]
    rank_in_tile = jnp.sum((same_tile & earlier).astype(jnp.int32), axis=1)
    slot_of_piece = target_tile * CAPACITY + rank_in_tile
    placing = jnp.arange(slot_count, dtype=jnp.int32)[:, None] == slot_of_piece[None, :]
    place_float = placing.astype(jnp.float32)
    place_int = placing.astype(jnp.int32)

    def place(values):
        moved = jnp.dot(place_float, values.reshape(pieces, flat_size), precision=HIGHEST)
        return moved.reshape(slot_count, rows_dev, block_width)

    sent_height = place(piece_height)
    sent_weight = place(piece_weight)
    sent_block = jnp.sum(place_int * tile_block[None, :], axis=1).astype(jnp.float32)
    sent_width = jnp.sum(place_int * piece_width[None, :], axis=1).astype(jnp.float32)
    next_first = passed_along(piece_height[:, :1, :], "lat", -1)
    sent_north = place(north_steps(piece_height, next_first))
    got_height, got_weight, got_north, got_block_f, got_width_f = (
        lax.all_to_all(sent_height, "lon", split_axis=0, concat_axis=0, tiled=True),
        lax.all_to_all(sent_weight, "lon", split_axis=0, concat_axis=0, tiled=True),
        lax.all_to_all(sent_north, "lon", split_axis=0, concat_axis=0, tiled=True),
        lax.all_to_all(sent_block, "lon", split_axis=0, concat_axis=0, tiled=True),
        lax.all_to_all(sent_width, "lon", split_axis=0, concat_axis=0, tiled=True),
    )
    got_block = got_block_f.astype(jnp.int32)
    got_width = got_width_f.astype(jnp.int32)
    terms = piece_terms(got_height, got_weight, got_width, got_north, row_global)
    stacked = jnp.stack(terms, axis=1)
    block_hot = (got_block[:, None] == jnp.arange(tile_blocks, dtype=jnp.int32)[None, :]).astype(
        jnp.float32
    )
    fields = jnp.einsum("sb,sqrj->qrbj", block_hot, stacked, precision=HIGHEST).reshape(
        6, rows_dev, COLS_DEV
    )
    weight_sum, height_sum, east_weight_sum, east_sum, north_weight_sum, north_sum = (
        fields[0],
        fields[1],
        fields[2],
        fields[3],
        fields[4],
        fields[5],
    )
    target_east = east_sum / (east_weight_sum + DAMPING)
    target_north = north_sum / (north_weight_sum + DAMPING)
    south_row = passed_along(target_north[-1:, :], "lat", 1)
    west_east = jnp.concatenate([jnp.zeros_like(target_east[:, :1]), target_east[:, :-1]], axis=1)
    south_target = jnp.concatenate([south_row, target_north[:-1]], axis=0)
    right_side = MU_DATA * height_sum - (target_east - west_east) - (target_north - south_target)
    diagonal = MU_DATA * weight_sum + RIDGE
    has_upper = (row_global < ROWS - 1)[:, None]
    has_lower = (row_global > 0)[:, None]
    solution_field = jnp.zeros_like(right_side)
    residual = right_side
    direction = right_side
    norm_now = squares(residual)
    for iteration in range(ITERS):
        image = operate(direction, diagonal, has_upper, has_lower)
        curvature = lax.psum(jnp.sum(direction * image), ("lon", "lat"))
        alpha = norm_now / curvature
        solution_field = solution_field + alpha * direction
        residual = residual - alpha * image
        norm_next = squares(residual)
        direction = residual + norm_next / norm_now * direction
        norm_now = norm_next
    return (solution_field, residual)


def solution(mesh):
    return jax.shard_map(
        body,
        mesh=mesh,
        in_specs=(P("lon", "lat", None), P("lon", "lat", None), P("lon"), P("lon")),
        out_specs=(P("lat", "lon"), P("lat", "lon")),
        check_vma=False,
    )
```

profile of v0, /device:TPU:0, one launch (start us, length us, event | category | flops | bytes accessed | tf_op | source)
XLA Modules:
  0.0 428.8 jit_solution(17067550917423036836)
XLA Ops:
  2.9 7.3 %all-to-all-start = ((f32[8,2,1]{1,2,0:T(1,128)}), f32[8,2,1]{1,2,0:T(1,128)S(1)}, u32[]{:S(2)}, u32[]{:S(2)}) async-start(f32[8,2,1]{1,2,0:T(1,128)} %bitcast), calls=%async_computation | async-start | bytes 8192 | tf_op jit(solution)/shard_map/all_to_all | solution.py:109
  18.1 6.0 %all-to-all-start.4 = ((f32[8,2,1]{1,2,0:T(1,128)}), f32[8,2,1]{1,2,0:T(1,128)S(1)}, u32[]{:S(2)}, u32[]{:S(2)}) async-start(f32[8,2,1]{1,2,0:T(1,128)} %bitcast.14), calls=%async_computation.4 | async-start | bytes 8192 | tf_op jit(solution)/shard_map/all_to_all | solution.py:108
  24.2 6.4 %all-to-all-done.4 = f32[8,2,1]{1,2,0:T(1,128)S(1)} async-done(((f32[8,2,1]{1,2,0:T(1,128)}), f32[8,2,1]{1,2,0:T(1,128)S(1)}, u32[]{:S(2)}, u32[]{:S(2)}) %all-to-all-start.4) | async-done | bytes 96 | tf_op jit(solution)/shard_map/all_to_all | solution.py:108
  30.5 3.4 all-to-all-start.2
  34.9 8.0 %all-to-all-done.2 = f32[16,32,128]{2,1,0:T(8,128)S(1)} async-done(((f32[16,32,128]{2,1,0:T(8,128)}), f32[16,32,128]{2,1,0:T(8,128)S(1)}, u32[]{:S(2)}, u32[]{:S(2)}) %all-to-all-start.2) | async-done | bytes 262176 | tf_op jit(solution)/shard_map/all_to_all | solution.py:105
  43.0 3.6 all-to-all-start.1
  48.0 7.2 %all-to-all-done.1 = f32[16,32,128]{2,1,0:T(8,128)S(1)} async-done(((f32[16,32,128]{2,1,0:T(8,128)}), f32[16,32,128]{2,1,0:T(8,128)S(1)}, u32[]{:S(2)}, u32[]{:S(2)}) %all-to-all-start.1) | async-done | bytes 262176 | tf_op jit(solution)/shard_map/all_to_all | solution.py:106
  55.1 3.6 all-to-all-start.3
  59.8 7.5 %all-to-all-done.3 = f32[16,32,128]{2,1,0:T(8,128)S(1)} async-done(((f32[16,32,128]{2,1,0:T(8,128)}), f32[16,32,128]{2,1,0:T(8,128)S(1)}, u32[]{:S(2)}, u32[]{:S(2)}) %all-to-all-start.3) | async-done | bytes 262176 | tf_op jit(solution)/shard_map/all_to_all | solution.py:107
  73.0 2.3 collective-permute-start.3
  76.8 4.9 %collective-permute-done.2 = f32[32,1]{1,0:T(8,128)S(1)} collective-permute-done((f32[32,1]{1,0:T(8,128)S(1)}, f32[32,1]{1,0:T(8,128)S(1)}, u32[]{:S(2)}, u32[]{:S(2)}) %collective-permute-start.2) | collective-permute-done | bytes 160 | tf_op jit(solution)/shard_map/ppermute | solution.py:24
  84.0 3.9 collective-permute-done.5
  89.2 37.2 %all-reduce.2 = (f32[]{:T(128)}, f32[]{:T(128)}) all-reduce(f32[]{:T(128)} %get-tuple-element.3, f32[]{:T(128)} %get-tuple-element.2), channel_id=1, replica_groups=mesh['lon'=8,'lat'=4] {'lon','lat'}, use_global_device_ids=true, to_apply=%region_4.5 | all-reduce | flops 2 | bytes 16 | tf_op jit(solution)/shard_map/psum | solution.py:73
  128.5 42.8 %psum.58 = f32[]{:T(128)} all-reduce(f32[]{:T(128)} %multiply_reduce_fusion.5), channel_id=1, replica_groups=mesh['lon'=8,'lat'=4] {'lon','lat'}, use_global_device_ids=true, to_apply=%region_8.9 | all-reduce | flops 1 | bytes 8 | tf_op jit(solution)/shard_map/psum | solution.py:73
  172.8 3.3 collective-permute-start.7
  177.5 5.0 %collective-permute-done.6 = f32[32,1]{1,0:T(8,128)S(1)} collective-permute-done((f32[32,1]{1,0:T(8,128)S(1)}, f32[32,1]{1,0:T(8,128)S(1)}, u32[]{:S(2)}, u32[]{:S(2)}) %collective-permute-start.6) | collective-permute-done | bytes 160 | tf_op jit(solution)/shard_map/ppermute | solution.py:24
  184.3 2.0 collective-permute-done.9
  187.6 37.1 %psum.59 = f32[]{:T(128)} all-reduce(f32[]{:T(128)} %get-tuple-element.16), channel_id=1, replica_groups=mesh['lon'=8,'lat'=4] {'lon','lat'}, use_global_device_ids=true, to_apply=%region_10.11 | all-reduce | flops 1 | bytes 8 | tf_op jit(solution)/shard_map/psum | solution.py:144
  226.7 41.7 %psum.60 = f32[]{:T(128)} all-reduce(f32[]{:T(128)} %get-tuple-element.14), channel_id=1, replica_groups=mesh['lon'=8,'lat'=4] {'lon','lat'}, use_global_device_ids=true, to_apply=%region_12.13 | all-reduce | flops 1 | bytes 8 | tf_op jit(solution)/shard_map/psum | solution.py:73
  269.9 3.3 collective-permute-start.11
  274.7 5.0 %collective-permute-done.10 = f32[32,1]{1,0:T(8,128)S(1)} collective-permute-done((f32[32,1]{1,0:T(8,128)S(1)}, f32[32,1]{1,0:T(8,128)S(1)}, u32[]{:S(2)}, u32[]{:S(2)}) %collective-permute-start.10) | collective-permute-done | bytes 160 | tf_op jit(solution)/shard_map/ppermute | solution.py:24
  281.6 1.8 collective-permute-done.13
  283.4 2.2 multiply_reduce_fusion.2
  285.6 37.1 %psum.61 = f32[]{:T(128)} all-reduce(f32[]{:T(128)} %get-tuple-element.12), channel_id=1, replica_groups=mesh['lon'=8,'lat'=4] {'lon','lat'}, use_global_device_ids=true, to_apply=%region_14.15 | all-reduce | flops 1 | bytes 8 | tf_op jit(solution)/shard_map/psum | solution.py:144
  324.0 1.9 multiply_reduce_fusion.1
  325.8 42.8 %psum.62 = f32[]{:T(128)} all-reduce(f32[]{:T(128)} %get-tuple-element.10), channel_id=1, replica_groups=mesh['lon'=8,'lat'=4] {'lon','lat'}, use_global_device_ids=true, to_apply=%region_16.17 | all-reduce | flops 1 | bytes 8 | tf_op jit(solution)/shard_map/psum | solution.py:73
  370.0 3.3 collective-permute-start.15
  374.7 5.0 %collective-permute-done.14 = f32[32,1]{1,0:T(8,128)S(1)} collective-permute-done((f32[32,1]{1,0:T(8,128)S(1)}, f32[32,1]{1,0:T(8,128)S(1)}, u32[]{:S(2)}, u32[]{:S(2)}) %collective-permute-start.14) | collective-permute-done | bytes 160 | tf_op jit(solution)/shard_map/ppermute | solution.py:24
  383.2 1.8 collective-permute-done.17
  385.0 3.3 multiply_reduce_fusion
  388.3 37.1 %psum.63 = f32[]{:T(128)} all-reduce(f32[]{:T(128)} %get-tuple-element.8), channel_id=1, replica_groups=mesh['lon'=8,'lat'=4] {'lon','lat'}, use_global_device_ids=true, to_apply=%region_18.19 | all-reduce | flops 1 | bytes 8 | tf_op jit(solution)/shard_map/psum | solution.py:144
  426.6 2.2 multiply_subtract_fusion
  (86 shorter events, 39.1 us)
Async XLA Ops:
  2.9 15.2 %all-to-all-start = ((f32[8,2,1]{1,2,0:T(1,128)}), f32[8,2,1]{1,2,0:T(1,128)S(1)}, u32[]{:S(2)}, u32[]{:S(2)}) async-start(f32[8,2,1]{1,2,0:T(1,128)} %bitcast), calls=%async_computation | async-start | bytes 8192 | tf_op jit(solution)/shard_map/all_to_all | solution.py:109
  10.9 23.2 %collective-permute-start = (f32[8,1,128]{2,1,0:T(1,128)S(1)}, f32[8,1,128]{2,1,0:T(1,128)S(1)}, u32[]{:S(2)}, u32[]{:S(2)}) collective-permute-start(f32[8,1,128]{2,1,0:T(1,128)S(1)} %slice.173), channel_id=1, source_target_pairs={{1,0},{2,1},{3,2},{5,4},{6,5},{7,6},{9,8},{10,9},{11,10},{13,12},{... | collective-permute-start | bytes 12296 | tf_op jit(solution)/shard_map/ppermute | solution.py:35
  18.1 12.5 %all-to-all-start.4 = ((f32[8,2,1]{1,2,0:T(1,128)}), f32[8,2,1]{1,2,0:T(1,128)S(1)}, u32[]{:S(2)}, u32[]{:S(2)}) async-start(f32[8,2,1]{1,2,0:T(1,128)} %bitcast.14), calls=%async_computation.4 | async-start | bytes 8192 | tf_op jit(solution)/shard_map/all_to_all | solution.py:108
  30.5 12.4 %all-to-all-start.2 = ((f32[16,32,128]{2,1,0:T(8,128)}), f32[16,32,128]{2,1,0:T(8,128)S(1)}, u32[]{:S(2)}, u32[]{:S(2)}) async-start(f32[16,32,128]{2,1,0:T(8,128)} %copy.21), calls=%async_computation.2 | async-start | bytes 524288 | tf_op jit(solution)/shard_map/all_to_all | solution.py:105
  43.0 12.2 %all-to-all-start.1 = ((f32[16,32,128]{2,1,0:T(8,128)}), f32[16,32,128]{2,1,0:T(8,128)S(1)}, u32[]{:S(2)}, u32[]{:S(2)}) async-start(f32[16,32,128]{2,1,0:T(8,128)} %copy.19), calls=%async_computation.1 | async-start | bytes 524288 | tf_op jit(solution)/shard_map/all_to_all | solution.py:106
  55.1 12.1 %all-to-all-start.3 = ((f32[16,32,128]{2,1,0:T(8,128)}), f32[16,32,128]{2,1,0:T(8,128)S(1)}, u32[]{:S(2)}, u32[]{:S(2)}) async-start(f32[16,32,128]{2,1,0:T(8,128)} %copy.27), calls=%async_computation.3 | async-start | bytes 524288 | tf_op jit(solution)/shard_map/all_to_all | solution.py:107
  69.5 2.1 collective-permute-start.1
  73.0 3.7 collective-permute-start.3
  75.3 6.4 %collective-permute-start.2 = (f32[32,1]{1,0:T(8,128)S(1)}, f32[32,1]{1,0:T(8,128)S(1)}, u32[]{:S(2)}, u32[]{:S(2)}) collective-permute-start(f32[32,1]{1,0:T(8,128)S(1)} %get-tuple-element.38), channel_id=1, source_target_pairs={{0,4},{4,8},{8,12},{12,16},{16,20},{20,24},{24,28},{28,0},{1,5},{5... | collective-permute-start | bytes 392 | tf_op jit(solution)/shard_map/ppermute | solution.py:24
  82.1 1.9 collective-permute-start.4
  82.5 5.3 %collective-permute-start.5 = (f32[1,4098]{1,0:T(1,128)S(1)}, f32[1,4098]{1,0:T(1,128)S(1)}, u32[]{:S(2)}, u32[]{:S(2)}) collective-permute-start(f32[1,4098]{1,0:T(1,128)S(1)} %get-tuple-element.30), channel_id=1, source_target_pairs={{0,1},{1,2},{2,3},{3,0},{4,5},{5,6},{6,7},{7,4},{8,9},{9,10},{10,1... | collective-permute-start | bytes 49184 | tf_op jit(solution)/shard_map/ppermute | solution.py:24
  172.8 4.7 %collective-permute-start.7 = (f32[32,1]{1,0:T(8,128)S(1)}, f32[32,1]{1,0:T(8,128)S(1)}, u32[]{:S(2)}, u32[]{:S(2)}) collective-permute-start(f32[32,1]{1,0:T(8,128)S(1)} %get-tuple-element.35), channel_id=1, source_target_pairs={{4,0},{8,4},{12,8},{16,12},{20,16},{24,20},{28,24},{0,28},{5,1},{9... | collective-permute-start | bytes 392 | tf_op jit(solution)/shard_map/ppermute | solution.py:27
  176.0 6.4 %collective-permute-start.6 = (f32[32,1]{1,0:T(8,128)S(1)}, f32[32,1]{1,0:T(8,128)S(1)}, u32[]{:S(2)}, u32[]{:S(2)}) collective-permute-start(f32[32,1]{1,0:T(8,128)S(1)} %get-tuple-element.36), channel_id=1, source_target_pairs={{0,4},{4,8},{8,12},{12,16},{16,20},{20,24},{24,28},{28,0},{1,5},{5... | collective-permute-start | bytes 392 | tf_op jit(solution)/shard_map/ppermute | solution.py:24
  182.8 1.5 collective-permute-start.8
  182.9 3.4 collective-permute-start.9
  269.9 4.8 %collective-permute-start.11 = (f32[32,1]{1,0:T(8,128)S(1)}, f32[32,1]{1,0:T(8,128)S(1)}, u32[]{:S(2)}, u32[]{:S(2)}) collective-permute-start(f32[32,1]{1,0:T(8,128)S(1)} %get-tuple-element.33), channel_id=1, source_target_pairs={{4,0},{8,4},{12,8},{16,12},{20,16},{24,20},{28,24},{0,28},{5,1},{9... | collective-permute-start | bytes 392 | tf_op jit(solution)/shard_map/ppermute | solution.py:27
  273.3 6.4 %collective-permute-start.10 = (f32[32,1]{1,0:T(8,128)S(1)}, f32[32,1]{1,0:T(8,128)S(1)}, u32[]{:S(2)}, u32[]{:S(2)}) collective-permute-start(f32[32,1]{1,0:T(8,128)S(1)} %get-tuple-element.34), channel_id=1, source_target_pairs={{0,4},{4,8},{8,12},{12,16},{16,20},{20,24},{24,28},{28,0},{1,5},{5... | collective-permute-start | bytes 392 | tf_op jit(solution)/shard_map/ppermute | solution.py:24
  280.1 1.5 collective-permute-start.12
  280.1 3.3 collective-permute-start.13
  370.0 4.7 %collective-permute-start.15 = (f32[32,1]{1,0:T(8,128)S(1)}, f32[32,1]{1,0:T(8,128)S(1)}, u32[]{:S(2)}, u32[]{:S(2)}) collective-permute-start(f32[32,1]{1,0:T(8,128)S(1)} %get-tuple-element.31), channel_id=1, source_target_pairs={{4,0},{8,4},{12,8},{16,12},{20,16},{24,20},{28,24},{0,28},{5,1},{9... | collective-permute-start | bytes 392 | tf_op jit(solution)/shard_map/ppermute | solution.py:27
  373.2 6.4 %collective-permute-start.14 = (f32[32,1]{1,0:T(8,128)S(1)}, f32[32,1]{1,0:T(8,128)S(1)}, u32[]{:S(2)}, u32[]{:S(2)}) collective-permute-start(f32[32,1]{1,0:T(8,128)S(1)} %get-tuple-element.32), channel_id=1, source_target_pairs={{0,4},{4,8},{8,12},{12,16},{16,20},{20,24},{24,28},{28,0},{1,5},{5... | collective-permute-start | bytes 392 | tf_op jit(solution)/shard_map/ppermute | solution.py:24
  381.7 1.5 collective-permute-start.16
  381.7 3.2 collective-permute-start.17
where the time goes:
time: 431 us; the launch traced here: 429 us
  blocking collectives  276 us (64%)
  waiting for transfers between devices  68.4 us (16%)
  starting transfers between devices  40.9 us (9%)
  other arithmetic  20.4 us (5%)
  between operations  10.1 us (2%)
  local copies, waits for them, and re-layouts  8.78 us (2%)
  matrix products  4.46 us (1%)
    psum x4, blocking collectives, squares(): return lax.psum(jnp.sum(residual * residual), ('lon', 'lat'))  165 us
    psum x3, blocking collectives, body(): curvature = lax.psum(jnp.sum(direction * image), ('lon', 'lat'))  111 us
    ppermute x8, waiting for transfers between devices, padded_2(): lax.ppermute(lax.slice_in_dim(block, block.shape[dim] - width, None, axis...  29.4 us
    ppermute x8, starting transfers between devices, padded_2(): lax.ppermute(lax.slice_in_dim(block, 0, width, axis=dim), axis, backward)  12.8 us
    ppermute x8, waiting for transfers between devices, padded_2(): lax.ppermute(lax.slice_in_dim(block, 0, width, axis=dim), axis, backward)  9.83 us
  transfers between devices with their start and end apart: 23, of which 21 were waited for; matrix products, arithmetic and copies ran while one was open for 3% of the time, Pallas kernels for 0%

commit v1 on v0

v1 whole, which is shorter than its diff:
```python
import functools

import jax
import jax.numpy as jnp
from jax import lax
from jax.experimental import pallas as pl
from jax.experimental.pallas import tpu as pltpu
from jax.sharding import PartitionSpec as P

COLS_DEV = 4096
ITERS = 4
MU_DATA = 0.5
DAMPING = 0.5
RIDGE = 0.05
SHIFT = 5.0
SCALE = 5.0

LANES = 128
MESH = pl.DeviceIdType.MESH
F32 = jnp.float32


def remote(src, dst, send, recv, device):
    return pltpu.make_async_remote_copy(
        src_ref=src, dst_ref=dst, send_sem=send, recv_sem=recv,
        device_id=device, device_id_type=MESH,
    )


def cg_coefficients(mu):
    def inner(a, b):
        total = None
        for i, x in enumerate(a):
            for j, y in enumerate(b):
                term = x * y * mu[i + j]
                total = term if total is None else total + term
        return total

    def apply(c):
        out = [SHIFT * x for x in c] + [jnp.zeros_like(c[0])]
        for i, x in enumerate(c):
            out[i + 1] = out[i + 1] + SCALE * x
        return out

    def add_scaled(y, a, x):
        out = []
        for i in range(max(len(x), len(y))):
            if i >= len(y):
                out.append(a * x[i])
            elif i >= len(x):
                out.append(y[i])
            else:
                out.append(y[i] + a * x[i])
        return out

    one = jnp.ones_like(mu[0])
    residual, direction, field = [one], [one], []
    norm = mu[0]
    for step in range(ITERS):
        image = apply(direction)
        alpha = norm / inner(direction, image)
        field = add_scaled(field, alpha, direction)
        residual = add_scaled(residual, -alpha, image)
        if step < ITERS - 1:
            fresh = inner(residual, residual)
            direction = add_scaled(residual, fresh / norm, direction)
            norm = fresh
    return field, residual


def kernel(
    n, lats, pieces, rows,
    col_ref, wid_ref, h_ref, w_ref, x_ref, r_ref,
    hs, ws, hr, wr, ms, mr, msm, idx_s, up_s, up_r, dn_s, dn_r,
    blk_s, prev_s, last_v, last_s, S,
    V, D, east_s, east_r, west_s, west_r, lat_up_s, lat_up_r, lat_dn_s, lat_dn_r,
    red, ra, rb,
    sem_m, sem_h, sem_w, sem_e, sem_l, sem_t, sem_a, sem_b, sem_loc,
):
    lon = lax.axis_index("lon")
    lat = lax.axis_index("lat")
    blocks = COLS_DEV // LANES
    ext = blocks + 2
    top = rows + 8
    slots = 2 * n
    lane = lax.broadcasted_iota(jnp.int32, (rows, LANES), 1)
    lane1 = lax.broadcasted_iota(jnp.int32, (1, LANES), 1)

    def lon_at(k):
        return lax.rem(lon + k, n)

    def lat_at(k):
        return lax.rem(lat + k, lats)

    barrier = pltpu.get_barrier_semaphore()

    @pl.loop(1, n)
    def _(k):
        pl.semaphore_signal(barrier, inc=1, device_id=(lon_at(k), lat), device_id_type=MESH)

    @pl.loop(1, lats)
    def _(k):
        pl.semaphore_signal(barrier, inc=1, device_id=(lon, lat_at(k)), device_id_type=MESH)

    @pl.loop(0, pieces)
    def _(i):
        up_s[0, pl.ds(i, 1), :] = h_ref[i, rows - 1 : rows, :]
        up_s[1, pl.ds(i, 1), :] = w_ref[i, rows - 1 : rows, :]
        dn_s[pl.ds(i, 1), :] = h_ref[i, 0:1, :]

    def fill(k, h_to, w_to, m_to):
        dest = lon_at(k)

        def scan(i, found):
            first, second = found
            match = (col_ref[i] >> 12) == dest
            second = jnp.where(match & (first >= 0) & (second < 0), i, second)
            first = jnp.where(match & (first < 0), i, first)
            return first, second

        found = lax.fori_loop(0, pieces, scan, (jnp.int32(-1), jnp.int32(-1)), unroll=8)
        tags = []
        for q in range(2):
            at = jnp.maximum(found[q], 0)
            limit = jnp.where(found[q] >= 0, wid_ref[at], 0)
            tags.append(jnp.where(found[q] >= 0, (col_ref[at] >> 7) & (blocks - 1), -1))
            idx_s[k, q] = at
            idx_s[k, 2 + q] = limit
            h_to[k, q * rows : (q + 1) * rows, :] = h_ref[at]
            w_to[k, q * rows : (q + 1) * rows, :] = jnp.where(lane < limit, w_ref[at], 0.0)
        m_to[k] = jnp.where(lane1 == 0, tags[0], jnp.where(lane1 == 1, tags[1], -1))

    fill(0, hr, wr, mr)

    @pl.loop(1, n)
    def _(k):
        fill(k, hs, ws, ms)

    pl.semaphore_wait(barrier, n - 1 + lats - 1)

    def edge_up():
        return remote(up_s, up_r, sem_e.at[0], sem_e.at[1], (lon, lat_at(1)))

    def edge_dn():
        return remote(dn_s, dn_r, sem_e.at[2], sem_e.at[3], (lon, lat_at(lats - 1)))

    def meta(k):
        return remote(ms.at[k], mr.at[k], sem_m.at[0, k], sem_m.at[1, k], (lon_at(k), lat))

    def heights(k):
        return remote(hs.at[k], hr.at[k], sem_h.at[0, k], sem_h.at[1, k], (lon_at(k), lat))

    def weights(k):
        return remote(ws.at[k], wr.at[k], sem_w.at[0, k], sem_w.at[1, k], (lon_at(k), lat))

    @pl.when(lat < lats - 1)
    def _():
        edge_up().start()

    @pl.when(lat > 0)
    def _():
        edge_dn().start()

    @pl.loop(1, n)
    def _(k):
        meta(k).start()

    @pl.loop(1, n)
    def _(k):
        heights(k).start()

    @pl.when(lat > 0)
    def _():
        edge_up().wait_recv()

    @pl.when(lat == 0)
    def _():
        up_r[...] = jnp.zeros_like(up_r)

    @pl.when(lat < lats - 1)
    def _():
        edge_dn().wait_recv()

    @pl.when(lat == lats - 1)
    def _():
        dn_r[...] = jnp.zeros_like(dn_r)

    def extras(k, w_to):
        for q in range(2):
            at, limit = idx_s[k, q], idx_s[k, 2 + q]
            base = 2 * rows + q
            w_to[k, base : base + 1, :] = dn_r[pl.ds(at, 1), :]
            w_to[k, base + 2 : base + 3, :] = up_r[0, pl.ds(at, 1), :]
            w_to[k, base + 4 : base + 5, :] = jnp.where(lane1 < limit, up_r[1, pl.ds(at, 1), :], 0.0)
        w_to[k, 2 * rows + 6 : 2 * rows + 8, :] = jnp.zeros((2, LANES), F32)

    @pl.loop(1, n)
    def _(k):
        extras(k, ws)
        weights(k).start()

    extras(0, wr)

    @pl.loop(1, n)
    def _(k):
        meta(k).wait_recv()

    tags_in = pltpu.make_async_copy(mr, msm, sem_loc.at[0])
    tags_in.start()
    tags_in.wait()

    @pl.loop(0, n)
    def _(k):
        blk_s[2 * k] = msm[k, 0, 0]
        blk_s[2 * k + 1] = msm[k, 0, 1]

    def latest(p, last):
        tag = blk_s[p]

        def scan(j, found):
            return jnp.where((j < p) & (blk_s[j] == tag), j, found)

        prev_s[p] = lax.fori_loop(0, slots, scan, jnp.int32(slots), unroll=8)
        return jnp.where(lane1 == tag, p, last)

    last_v[...] = lax.fori_loop(0, slots, latest, jnp.full((1, LANES), slots, jnp.int32))
    last_in = pltpu.make_async_copy(last_v, last_s, sem_loc.at[1])
    last_in.start()
    last_in.wait()

    S[slots] = jnp.zeros((6 * rows + 8, LANES), F32)
    row_global = lat * rows + lax.broadcasted_iota(jnp.int32, (rows, LANES), 0)
    has_north = row_global < lats * rows - 1
    row_in = lax.broadcasted_iota(jnp.int32, (rows, LANES), 0)

    def terms(k):
        for q in range(2):
            p = 2 * k + q
            before = prev_s[p]
            h = hr[k, q * rows : (q + 1) * rows, :]
            w = wr[k, q * rows : (q + 1) * rows, :]
            base = 2 * rows + q
            above = wr[k, base : base + 1, :]
            below_h = wr[k, base + 2 : base + 3, :]
            below_w = wr[k, base + 4 : base + 5, :]
            h_north = jnp.where(row_in == rows - 1, above, pltpu.roll(h, rows - 1, 0))
            h_east = pltpu.roll(h, LANES - 1, 1)
            w_east = jnp.where((pltpu.roll(w, LANES - 1, 1) > 0.0) & (lane < LANES - 1), w, 0.0)
            w_north = jnp.where(has_north, w, 0.0)
            parts = (w, w * h, w_east, w_east * (h_east - h), w_north, w_north * (h_north - h))
            for t, part in enumerate(parts):
                at = pl.ds(t * rows, rows)
                S[p, at, :] = part + S[before, at, :]
            at = 6 * rows
            S[p, at : at + 1, :] = below_w + S[before, at : at + 1, :]
            S[p, at + 1 : at + 2, :] = below_w * (h[0:1, :] - below_h) + S[before, at + 1 : at + 2, :]

    terms(0)

    @pl.loop(1, n)
    def _(k):
        heights(k).wait_recv()
        weights(k).wait_recv()
        terms(k)

    inv = 1.0 / SCALE

    def assemble(b, before):
        p = last_s[0, b]

        def field(t):
            return S[p, t * rows : (t + 1) * rows, :]

        at = 6 * rows
        t_east = field(3) / (field(2) + DAMPING)
        t_north = field(5) / (field(4) + DAMPING)
        t_below = S[p, at + 1 : at + 2, :] / (S[p, at : at + 1, :] + DAMPING)
        t_south = jnp.where(row_in == 0, t_below, pltpu.roll(t_north, 1, 0))
        rolled = pltpu.roll(t_east, 1, 1)
        t_west = jnp.where(lane == 0, before, rolled)
        right = MU_DATA * field(1) - (t_east - t_west) - (t_north - t_south)
        cols = pl.ds(pl.multiple_of((b + 1) * LANES, LANES), LANES)
        V[0, 8:top, cols] = right
        D[8:top, cols] = (MU_DATA * field(0) + (RIDGE + 4.0 - SHIFT)) * inv
        return rolled

    east_last = lax.fori_loop(0, blocks, assemble, jnp.zeros((rows, LANES), F32), unroll=2)

    first = slice(LANES, 2 * LANES)
    final = slice(blocks * LANES, (blocks + 1) * LANES)
    east_s[0:rows, :] = V[0, 8:top, final]
    east_s[rows : 2 * rows, :] = D[8:top, final]
    east_s[2 * rows : 3 * rows, :] = east_last
    west_s[0:rows, :] = V[0, 8:top, first]
    west_s[rows : 2 * rows, :] = D[8:top, first]
    east = remote(east_s, east_r, sem_l.at[0], sem_l.at[1], (lon_at(1), lat))
    west = remote(west_s, west_r, sem_l.at[2], sem_l.at[3], (lon_at(n - 1), lat))
    east.start()
    west.start()
    east.wait_recv()
    halo_w = slice(0, LANES)
    halo_e = slice((blocks + 1) * LANES, (blocks + 2) * LANES)
    V[0, 8:top, halo_w] = east_r[0:rows, :]
    D[8:top, halo_w] = east_r[rows : 2 * rows, :]
    V[0, 8:top, first] = V[0, 8:top, first] + jnp.where(lane == 0, east_r[2 * rows : 3 * rows, :], 0.0)
    west.wait_recv()
    V[0, 8:top, halo_e] = west_r[0:rows, :] + jnp.where(lane == 0, east_last, 0.0)
    D[8:top, halo_e] = west_r[rows : 2 * rows, :]

    lat_up_s[0:4, :] = D[top - 4 : top, :]
    lat_up_s[4:8, :] = V[0, top - 4 : top, :]
    lat_dn_s[0:4, :] = V[0, 8:12, :]
    lat_dn_s[4:8, :] = D[8:12, :]

    def rows_up():
        return remote(lat_up_s, lat_up_r, sem_t.at[0], sem_t.at[1], (lon, lat_at(1)))

    def rows_dn():
        return remote(lat_dn_s, lat_dn_r, sem_t.at[2], sem_t.at[3], (lon, lat_at(lats - 1)))

    @pl.when(lat < lats - 1)
    def _():
        rows_up().start()

    @pl.when(lat > 0)
    def _():
        rows_dn().start()

    def mirror(k):
        @pl.when(lat == 0)
        def _():
            V[k, 7:8, :] = V[k, 8:9, :]

        @pl.when(lat == lats - 1)
        def _():
            V[k, top : top + 1, :] = V[k, top - 1 : top, :]

    @pl.when(lat > 0)
    def _():
        rows_up().wait_recv()
        got = lat_up_r[...]
        V[0, 0:8, :] = got
        D[0:8, :] = pltpu.roll(got, 4, 0)

    @pl.when(lat == 0)
    def _():
        V[0, 0:8, :] = jnp.zeros((8, ext * LANES), F32)
        D[0:8, :] = jnp.zeros((8, ext * LANES), F32)

    @pl.when(lat < lats - 1)
    def _():
        rows_dn().wait_recv()
        got = lat_dn_r[...]
        V[0, top : top + 8, :] = got
        D[top : top + 8, :] = pltpu.roll(got, 4, 0)

    @pl.when(lat == lats - 1)
    def _():
        V[0, top : top + 8, :] = jnp.zeros((8, ext * LANES), F32)
        D[top : top + 8, :] = jnp.zeros((8, ext * LANES), F32)

    mirror(0)

    tall = rows + 16
    lane_t = lax.broadcasted_iota(jnp.int32, (tall, LANES), 1)

    def at_block(b):
        return pl.ds(pl.multiple_of(b * LANES, LANES), LANES)

    def fold(value):
        total = value[0:8]
        for i in range(1, rows // 8):
            total = total + value[8 * i : 8 * i + 8]
        return total

    def apply(k):
        def one(b, here, before, ahead):
            nxt = V[k, :, at_block(jnp.minimum(b + 1, ext - 1))]
            ahead_next = pltpu.roll(nxt, LANES - 1, 1)
            rolled = pltpu.roll(here, 1, 1)
            sides = jnp.where(lane_t == 0, before, rolled)
            sides = sides + jnp.where(lane_t == LANES - 1, ahead_next, ahead)
            sides = sides + pltpu.roll(here, 1, 0) + pltpu.roll(here, tall - 1, 0)
            out = D[:, at_block(b)] * here - inv * sides
            V[k + 1, :, at_block(b)] = out
            return out, nxt, rolled, ahead_next

        def step(b, carry):
            here, before, ahead, cross, own, base = carry
            out, nxt, rolled, ahead_next = one(b, here, before, ahead)
            mine, image = here[8:top], out[8:top]
            cross = cross + fold(mine * image)
            own = own + fold(image * image)
            if k == 0:
                base = base + fold(mine * mine)
            return nxt, rolled, ahead_next, cross, own, base

        here = V[k, :, 0:LANES]
        ahead = pltpu.roll(here, LANES - 1, 1)
        _, here, before, ahead = one(0, here, ahead, ahead)
        zero = jnp.zeros((8, LANES), F32)
        here, before, ahead, cross, own, base = lax.fori_loop(
            1, blocks + 1, step, (here, before, ahead, zero, zero, zero), unroll=2
        )
        if k < ITERS - 1:
            one(ext - 1, here, before, ahead)
            mirror(k + 1)
        return cross, own, base

    sums = []
    for k in range(ITERS):
        cross, own, base = apply(k)
        if k == 0:
            sums.append(base)
        sums += [cross, own]

    red[...] = jnp.zeros_like(red)
    for i, value in enumerate(sums):
        red[i : i + 1, :] = jnp.sum(value, axis=0, keepdims=True)

    def over_lat(k):
        return remote(red, ra.at[lat], sem_a.at[0, k], sem_a.at[1, k], (lon, lat_at(k)))

    def over_lon(k):
        return remote(red, rb.at[lon], sem_b.at[0, k], sem_b.at[1, k], (lon_at(k), lat))

    @pl.loop(1, lats)
    def _(k):
        over_lat(k).start()

    ra[lat] = red[...]

    @pl.loop(1, lats)
    def _(k):
        over_lat(k).wait()

    total = ra[0]
    for i in range(1, lats):
        total = total + ra[i]
    red[...] = total

    @pl.loop(1, n)
    def _(k):
        over_lon(k).start()

    rb[lon] = red[...]

    @pl.loop(1, n)
    def _(k):
        over_lon(k).wait()

    total = rb[0]
    for i in range(1, n):
        total = total + rb[i]

    mu = [
        jnp.broadcast_to(jnp.sum(total[i : i + 1, :], axis=1, keepdims=True), (8, LANES))
        for i in range(2 * ITERS + 1)
    ]
    field, residual = cg_coefficients(mu)
    field = [jnp.concatenate([c] * (rows // 8), axis=0) for c in field]
    residual = [jnp.concatenate([c] * (rows // 8), axis=0) for c in residual]

    def combine(b, carry):
        cols = at_block(b + 1)
        v = V[0, 8:top, cols]
        x, r = field[0] * v, residual[0] * v
        for k in range(1, ITERS + 1):
            v = V[k, 8:top, cols]
            r = r + residual[k] * v
            if k < ITERS:
                x = x + field[k] * v
        x_ref[:, at_block(b)] = x
        r_ref[:, at_block(b)] = r
        return carry

    lax.fori_loop(0, blocks, combine, 0, unroll=2)

    @pl.loop(1, n)
    def _(k):
        meta(k).wait_send()
        heights(k).wait_send()
        weights(k).wait_send()

    east.wait_send()
    west.wait_send()

    @pl.when(lat < lats - 1)
    def _():
        edge_up().wait_send()
        rows_up().wait_send()

    @pl.when(lat > 0)
    def _():
        edge_dn().wait_send()
        rows_dn().wait_send()


def body(n, lats, piece_height, piece_weight, piece_column, piece_width):
    pieces, rows, width = piece_height.shape
    ext = COLS_DEV + 2 * LANES
    vmem = pltpu.VMEM
    dma = pltpu.SemaphoreType.DMA
    scratch = [
        vmem((n, 2 * rows, LANES), F32),
        vmem((n, 2 * rows + 8, LANES), F32),
        vmem((n, 2 * rows, LANES), F32),
        vmem((n, 2 * rows + 8, LANES), F32),
        vmem((n, 1, LANES), jnp.int32),
        vmem((n, 1, LANES), jnp.int32),
        pltpu.SMEM((n, 1, LANES), jnp.int32),
        pltpu.SMEM((n, 4), jnp.int32),
        vmem((2, pieces, LANES), F32),
        vmem((2, pieces, LANES), F32),
        vmem((pieces, LANES), F32),
        vmem((pieces, LANES), F32),
        pltpu.SMEM((2 * n,), jnp.int32),
        pltpu.SMEM((2 * n,), jnp.int32),
        vmem((1, LANES), jnp.int32),
        pltpu.SMEM((1, LANES), jnp.int32),
        vmem((2 * n + 1, 6 * rows + 8, LANES), F32),
        vmem((ITERS + 1, rows + 16, ext), F32),
        vmem((rows + 16, ext), F32),
        vmem((3 * rows, LANES), F32),
        vmem((3 * rows, LANES), F32),
        vmem((2 * rows, LANES), F32),
        vmem((2 * rows, LANES), F32),
        vmem((8, ext), F32),
        vmem((8, ext), F32),
        vmem((8, ext), F32),
        vmem((8, ext), F32),
        vmem((16, LANES), F32),
        vmem((lats, 16, LANES), F32),
        vmem((n, 16, LANES), F32),
        dma((2, n)),
        dma((2, n)),
        dma((2, n)),
        dma((4,)),
        dma((4,)),
        dma((4,)),
        dma((2, lats)),
        dma((2, n)),
        dma((2,)),
    ]
    out = jax.ShapeDtypeStruct((rows, COLS_DEV), F32)
    return pl.pallas_call(
        functools.partial(kernel, n, lats, pieces, rows),
        out_shape=(out, out),
        in_specs=[pl.BlockSpec(memory_space=pltpu.SMEM)] * 2 + [pl.BlockSpec(memory_space=pltpu.VMEM)] * 2,
        out_specs=(pl.BlockSpec(memory_space=pltpu.VMEM),) * 2,
        scratch_shapes=scratch,
        compiler_params=pltpu.CompilerParams(
            collective_id=0, has_side_effects=True, vmem_limit_bytes=48 * 1024 * 1024
        ),
    )(piece_column, piece_width, piece_height, piece_weight)


def solution(mesh):
    return jax.shard_map(
        functools.partial(body, mesh.shape["lon"], mesh.shape["lat"]),
        mesh=mesh,
        in_specs=(P("lon", "lat", None), P("lon", "lat", None), P("lon"), P("lon")),
        out_specs=(P("lat", "lon"), P("lat", "lon")),
        check_vma=False,
    )
```

time: 431 us -> 53 us (0.12)
  blocking collectives: 276 us -> 0 us
  waiting for transfers between devices: 68.4 us -> 0 us
  Pallas kernels: 0 us -> 47.5 us
  starting transfers between devices: 40.9 us -> 0 us
  other arithmetic: 20.4 us -> 0 us
  between operations: 10.1 us -> 0.65 us
  matrix products: 4.46 us -> 0 us
    psum x7 -> x0, blocking collectives: 276 us -> none  [the longest x4 165 us: squares(): return lax.psum(jnp.sum(residual * residual), ('lon', 'lat'))]
    pallas_call x0 -> x1, Pallas kernels: none -> 47.5 us  [body(): pl.pallas_call(functools.partial(kernel, n, lats, pieces, rows), out_shap...]
    ppermute x18 -> x0, waiting for transfers between devices: 39.3 us -> none  [the longest x8 29.4 us: padded_2(): lax.ppermute(lax.slice_in_dim(block, block.shape[dim] - width, None, axis...]
    all_to_all x5 -> x0, waiting for transfers between devices: 29 us -> none  [the longest x1 8.03 us: body(): lax.all_to_all(sent_height, 'lon', split_axis=0, concat_axis=0, tiled=True)]
    all_to_all x5 -> x0, starting transfers between devices: 23.8 us -> none  [the longest x1 7.25 us: body(): lax.all_to_all(sent_width, 'lon', split_axis=0, concat_axis=0, tiled=True)]
    ppermute x18 -> x0, starting transfers between devices: 17.1 us -> none  [the longest x8 12.8 us: padded_2(): lax.ppermute(lax.slice_in_dim(block, 0, width, axis=dim), axis, backward)]
    reduce_sum x9 -> x0, other arithmetic: 12.3 us -> none  [the longest x4 8.05 us: body(): curvature = lax.psum(jnp.sum(direction * image), ('lon', 'lat'))]
    sub x5 -> x0, other arithmetic: 5.41 us -> none  [the longest x1 2.18 us: body(): residual = residual - alpha * image]
  transfers between devices with their start and end apart: 23 -> 0, of which waited for: 21 -> 0; matrix products, arithmetic and copies ran while one was open for 3% -> 0% of each run, Pallas kernels for 0% -> 0%
where the time goes in v1:
time: 53 us; the launch traced here: 52.8 us
  Pallas kernels  47.5 us (90%)
  local copies, waits for them, and re-layouts  4.7 us (9%)
  between operations  0.65 us (1%)
    pallas_call x1, Pallas kernels, body(): pl.pallas_call(functools.partial(kernel, n, lats, pieces, rows), out_shap...  47.5 us
    unnamed x10, local copies, waits for them, and re-layouts  4.7 us

profile of v1, /device:TPU:0, one launch (start us, length us, event | category | flops | bytes accessed | tf_op | source)
XLA Modules:
  0.0 52.8 jit_solution(4659411516722245269)
XLA Ops:
  0.6 0.0 copy-start
  0.6 0.9 %copy-done = f32[8,32,128]{2,1,0:T(8,128)S(1)} copy-done((f32[8,32,128]{2,1,0:T(8,128)S(1)}, f32[8,32,128]{2,1,0:T(8,128)}, u32[]{:S(2)}) %copy-start) | copy-done | bytes 131096
  1.5 0.0 copy-start.1
  1.5 0.9 %copy-done.1 = f32[8,32,128]{2,1,0:T(8,128)S(1)} copy-done((f32[8,32,128]{2,1,0:T(8,128)S(1)}, f32[8,32,128]{2,1,0:T(8,128)}, u32[]{:S(2)}) %copy-start.1) | copy-done | bytes 131096
  2.4 0.0 copy-start.2
  2.4 0.7 %copy-done.2 = s32[8]{0:T(128)S(1)} copy-done((s32[8]{0:T(128)S(1)}, s32[8]{0:T(128)}, u32[]{:S(2)}) %copy-start.2) | copy-done | bytes 56
  3.1 0.0 copy-start.3
  3.1 0.7 %copy-done.3 = s32[8]{0:T(128)S(1)} copy-done((s32[8]{0:T(128)S(1)}, s32[8]{0:T(128)}, u32[]{:S(2)}) %copy-start.3) | copy-done | bytes 56
  3.8 47.5 %shard_map.59 = (f32[32,4096]{1,0:T(8,128)S(1)}, f32[32,4096]{1,0:T(8,128)S(1)}) custom-call(s32[8]{0:T(128)S(1)} %copy-done.2, s32[8]{0:T(128)S(1)} %copy-done.3, f32[8,32,128]{2,1,0:T(8,128)S(1)} %copy-done, f32[8,32,128]{2,1,0:T(8,128)S(1)} %copy-done.1), custom_call_target="tpu_custom_call" | custom-call | tf_op jit(solution)/shard_map/pallas_call | solution.py:546
  51.2 0.8 %copy.8 = f32[32,4096]{1,0:T(8,128)} copy(f32[32,4096]{1,0:T(8,128)S(1)} %get-tuple-element.4) | data formatting | bytes 1048576
  52.0 0.8 %copy.9 = f32[32,4096]{1,0:T(8,128)} copy(f32[32,4096]{1,0:T(8,128)S(1)} %get-tuple-element.5) | data formatting | bytes 1048576
Async XLA Ops:
  0.6 0.9 %copy-start = (f32[8,32,128]{2,1,0:T(8,128)S(1)}, f32[8,32,128]{2,1,0:T(8,128)}, u32[]{:S(2)}) copy-start(f32[8,32,128]{2,1,0:T(8,128)} %h_ref.1) | copy-start | bytes 393220
  1.5 0.9 %copy-start.1 = (f32[8,32,128]{2,1,0:T(8,128)S(1)}, f32[8,32,128]{2,1,0:T(8,128)}, u32[]{:S(2)}) copy-start(f32[8,32,128]{2,1,0:T(8,128)} %w_ref.1) | copy-start | bytes 393220
  2.4 0.7 %copy-start.2 = (s32[8]{0:T(128)S(1)}, s32[8]{0:T(128)}, u32[]{:S(2)}) copy-start(s32[8]{0:T(128)} %col_ref.1) | copy-start | bytes 100
  3.1 0.7 %copy-start.3 = (s32[8]{0:T(128)S(1)}, s32[8]{0:T(128)}, u32[]{:S(2)}) copy-start(s32[8]{0:T(128)} %wid_ref.1) | copy-start | bytes 100

commit v2 on v1

--- a/solution.py
+++ b/solution.py
@@ -16,6 +16,7 @@
 SCALE = 5.0
 
 LANES = 128
+CHUNKS = 4
 MESH = pl.DeviceIdType.MESH
 F32 = jnp.float32
 
@@ -70,10 +71,11 @@
 
 def kernel(
     n, lats, pieces, rows,
-    col_ref, wid_ref, h_ref, w_ref, x_ref, r_ref,
+    col_in, wid_in, h_in, w_in, V, coef_ref,
+    col_ref, wid_ref, h_ref, w_ref,
     hs, ws, hr, wr, ms, mr, msm, idx_s, up_s, up_r, dn_s, dn_r,
     blk_s, prev_s, last_v, last_s, S,
-    V, D, east_s, east_r, west_s, west_r, lat_up_s, lat_up_r, lat_dn_s, lat_dn_r,
+    D, east_s, east_r, west_s, west_r, lat_up_s, lat_up_r, lat_dn_s, lat_dn_r,
     red, ra, rb,
     sem_m, sem_h, sem_w, sem_e, sem_l, sem_t, sem_a, sem_b, sem_loc,
 ):
@@ -93,6 +95,14 @@
         return lax.rem(lat + k, lats)
 
     barrier = pltpu.get_barrier_semaphore()
+    loads = [
+        pltpu.make_async_copy(src, dst, sem_loc.at[2 + i])
+        for i, (src, dst) in enumerate(
+            ((col_in, col_ref), (wid_in, wid_ref), (h_in, h_ref), (w_in, w_ref))
+        )
+    ]
+    for load in loads:
+        load.start()
 
     @pl.loop(1, n)
     def _(k):
@@ -101,6 +111,9 @@
     @pl.loop(1, lats)
     def _(k):
         pl.semaphore_signal(barrier, inc=1, device_id=(lon, lat_at(k)), device_id_type=MESH)
+
+    for load in loads:
+        load.wait()
 
     @pl.loop(0, pieces)
     def _(i):
@@ -458,23 +471,8 @@
         for i in range(2 * ITERS + 1)
     ]
     field, residual = cg_coefficients(mu)
-    field = [jnp.concatenate([c] * (rows // 8), axis=0) for c in field]
-    residual = [jnp.concatenate([c] * (rows // 8), axis=0) for c in residual]
-
-    def combine(b, carry):
-        cols = at_block(b + 1)
-        v = V[0, 8:top, cols]
-        x, r = field[0] * v, residual[0] * v
-        for k in range(1, ITERS + 1):
-            v = V[k, 8:top, cols]
-            r = r + residual[k] * v
-            if k < ITERS:
-                x = x + field[k] * v
-        x_ref[:, at_block(b)] = x
-        r_ref[:, at_block(b)] = r
-        return carry
-
-    lax.fori_loop(0, blocks, combine, 0, unroll=2)
+    for i, c in enumerate(field + residual):
+        coef_ref[i : i + 1, :] = c[0:1, :]
 
     @pl.loop(1, n)
     def _(k):
@@ -494,6 +492,43 @@
     def _():
         edge_dn().wait_send()
         rows_dn().wait_send()
+
+
+def combine(rows, V, coef_ref, x_out, r_out, x_ref, r_ref, sem):
+    coef = [coef_ref[i : i + 1, :] for i in range(2 * ITERS + 1)]
+    coef = [jnp.broadcast_to(c, (rows, LANES)) for c in coef]
+    field, residual = coef[:ITERS], coef[ITERS:]
+    width = COLS_DEV // CHUNKS
+
+    def copies(c):
+        cols = pl.ds(c * width, width)
+        return (
+            pltpu.make_async_copy(x_ref.at[:, cols], x_out.at[:, cols], sem.at[0, c]),
+            pltpu.make_async_copy(r_ref.at[:, cols], r_out.at[:, cols], sem.at[1, c]),
+        )
+
+    for c in range(CHUNKS):
+
+        def one(b, carry):
+            v = V[0, 8 : rows + 8, pl.ds(pl.multiple_of((b + 1) * LANES, LANES), LANES)]
+            x, r = field[0] * v, residual[0] * v
+            for k in range(1, ITERS + 1):
+                v = V[k, 8 : rows + 8, pl.ds(pl.multiple_of((b + 1) * LANES, LANES), LANES)]
+                r = r + residual[k] * v
+                if k < ITERS:
+                    x = x + field[k] * v
+            cols = pl.ds(pl.multiple_of(b * LANES, LANES), LANES)
+            x_ref[:, cols] = x
+            r_ref[:, cols] = r
+            return carry
+
+        per = width // LANES
+        lax.fori_loop(c * per, (c + 1) * per, one, 0, unroll=4)
+        for copy in copies(c):
+            copy.start()
+    for c in range(CHUNKS):
+        for copy in copies(c):
+            copy.wait()
 
 
 def body(n, lats, piece_height, piece_weight, piece_column, piece_width):
@@ -502,6 +537,10 @@
     vmem = pltpu.VMEM
     dma = pltpu.SemaphoreType.DMA
     scratch = [
+        pltpu.SMEM((pieces,), jnp.int32),
+        pltpu.SMEM((pieces,), jnp.int32),
+        vmem((pieces, rows, LANES), F32),
+        vmem((pieces, rows, LANES), F32),
         vmem((n, 2 * rows, LANES), F32),
         vmem((n, 2 * rows + 8, LANES), F32),
         vmem((n, 2 * rows, LANES), F32),
@@ -519,7 +558,6 @@
         vmem((1, LANES), jnp.int32),
         pltpu.SMEM((1, LANES), jnp.int32),
         vmem((2 * n + 1, 6 * rows + 8, LANES), F32),
-        vmem((ITERS + 1, rows + 16, ext), F32),
         vmem((rows + 16, ext), F32),
         vmem((3 * rows, LANES), F32),
         vmem((3 * rows, LANES), F32),
@@ -540,19 +578,34 @@
         dma((4,)),
         dma((2, lats)),
         dma((2, n)),
-        dma((2,)),
+        dma((6,)),
     ]
-    out = jax.ShapeDtypeStruct((rows, COLS_DEV), F32)
-    return pl.pallas_call(
+    basis, coef = pl.pallas_call(
         functools.partial(kernel, n, lats, pieces, rows),
-        out_shape=(out, out),
-        in_specs=[pl.BlockSpec(memory_space=pltpu.SMEM)] * 2 + [pl.BlockSpec(memory_space=pltpu.VMEM)] * 2,
+        out_shape=(
+            jax.ShapeDtypeStruct((ITERS + 1, rows + 16, ext), F32),
+            jax.ShapeDtypeStruct((16, LANES), F32),
+        ),
+        in_specs=[pl.BlockSpec(memory_space=pltpu.HBM)] * 4,
         out_specs=(pl.BlockSpec(memory_space=pltpu.VMEM),) * 2,
         scratch_shapes=scratch,
         compiler_params=pltpu.CompilerParams(
             collective_id=0, has_side_effects=True, vmem_limit_bytes=48 * 1024 * 1024
         ),
-    )(piece_column, piece_width, piece_height, piece_weight)
+    )(*(pltpu.with_memory_space_constraint(a, pltpu.HBM) for a in (piece_column, piece_width, piece_height, piece_weight)))
+    out = jax.ShapeDtypeStruct((rows, COLS_DEV), F32)
+    return pl.pallas_call(
+        functools.partial(combine, rows),
+        out_shape=(out, out),
+        in_specs=[pl.BlockSpec(memory_space=pltpu.VMEM)] * 2,
+        out_specs=(pl.BlockSpec(memory_space=pltpu.HBM),) * 2,
+        scratch_shapes=[
+            vmem((rows, COLS_DEV), F32),
+            vmem((rows, COLS_DEV), F32),
+            dma((2, CHUNKS)),
+        ],
+        compiler_params=pltpu.CompilerParams(vmem_limit_bytes=16 * 1024 * 1024),
+    )(basis, coef)
 
 
 def solution(mesh):

time: 53 us -> 48.5 us (0.915)
  local copies, waits for them, and re-layouts: 4.7 us -> 0 us
    unnamed x10 -> x0, local copies, waits for them, and re-layouts: 4.7 us -> none
    pallas_call x0 -> x1, Pallas kernels: none -> 1.1 us  [body(): pl.pallas_call(functools.partial(combine, rows), out_shape=(out, out), in...]
    pallas_call x1, Pallas kernels: 47.5 us -> 46.6 us  [body(): pl.pallas_call(functools.partial(kernel, n, lats, pieces, rows), out_shap...]
where the time goes in v2:
time: 48.5 us; the launch traced here: 48.3 us
  Pallas kernels  47.7 us (98%)
  between operations  0.64 us (1%)
    pallas_call x1, Pallas kernels, body(): pl.pallas_call(functools.partial(kernel, n, lats, pieces, rows), out_shap...  46.6 us
    pallas_call x1, Pallas kernels, body(): pl.pallas_call(functools.partial(combine, rows), out_shape=(out, out), in...  1.1 us

profile of v2, /device:TPU:0, one launch (start us, length us, event | category | flops | bytes accessed | tf_op | source)
XLA Modules:
  0.0 48.3 jit_solution(9512498723698683637)
XLA Ops:
  0.6 46.6 %shard_map.59 = (f32[5,48,4352]{2,1,0:T(8,128)S(1)}, f32[16,128]{1,0:T(8,128)S(1)}) custom-call(s32[8]{0:T(128)} %col_in.1, s32[8]{0:T(128)} %wid_in.1, f32[8,32,128]{2,1,0:T(8,128)} %h_in.1, f32[8,32,128]{2,1,0:T(8,128)} %w_in.1), custom_call_target="tpu_custom_call" | custom-call | tf_op jit(solution)/shard_map/pallas_call | solution.py:583
  47.2 1.1 %shard_map.60 = (f32[32,4096]{1,0:T(8,128)}, f32[32,4096]{1,0:T(8,128)}) custom-call(f32[5,48,4352]{2,1,0:T(8,128)S(1)} %get-tuple-element.4.V, f32[16,128]{1,0:T(8,128)S(1)} %get-tuple-element.5.coef_ref), custom_call_target="tpu_custom_call" | custom-call | tf_op jit(solution)/shard_map/pallas_call | solution.py:597

commit v3 on v2

--- a/solution.py
+++ b/solution.py
@@ -91,6 +91,13 @@
     def lon_at(k):
         return lax.rem(lon + k, n)
 
+    def partner(k):
+        other, bit = jnp.int32(0), 1
+        while bit < n:
+            other = other + (lon // bit + k // bit) % 2 * bit
+            bit *= 2
+        return other
+
     def lat_at(k):
         return lax.rem(lat + k, lats)
 
@@ -106,7 +113,7 @@
 
     @pl.loop(1, n)
     def _(k):
-        pl.semaphore_signal(barrier, inc=1, device_id=(lon_at(k), lat), device_id_type=MESH)
+        pl.semaphore_signal(barrier, inc=1, device_id=(partner(k), lat), device_id_type=MESH)
 
     @pl.loop(1, lats)
     def _(k):
@@ -122,7 +129,7 @@
         dn_s[pl.ds(i, 1), :] = h_ref[i, 0:1, :]
 
     def fill(k, h_to, w_to, m_to):
-        dest = lon_at(k)
+        dest = partner(k)
 
         def scan(i, found):
             first, second = found
@@ -147,7 +154,7 @@
 
     @pl.loop(1, n)
     def _(k):
-        fill(k, hs, ws, ms)
+        fill(n - k, hs, ws, ms)
 
     pl.semaphore_wait(barrier, n - 1 + lats - 1)
 
@@ -158,13 +165,13 @@
         return remote(dn_s, dn_r, sem_e.at[2], sem_e.at[3], (lon, lat_at(lats - 1)))
 
     def meta(k):
-        return remote(ms.at[k], mr.at[k], sem_m.at[0, k], sem_m.at[1, k], (lon_at(k), lat))
+        return remote(ms.at[k], mr.at[k], sem_m.at[0, k], sem_m.at[1, k], (partner(k), lat))
 
     def heights(k):
-        return remote(hs.at[k], hr.at[k], sem_h.at[0, k], sem_h.at[1, k], (lon_at(k), lat))
+        return remote(hs.at[k], hr.at[k], sem_h.at[0, k], sem_h.at[1, k], (partner(k), lat))
 
     def weights(k):
-        return remote(ws.at[k], wr.at[k], sem_w.at[0, k], sem_w.at[1, k], (lon_at(k), lat))
+        return remote(ws.at[k], wr.at[k], sem_w.at[0, k], sem_w.at[1, k], (partner(k), lat))
 
     @pl.when(lat < lats - 1)
     def _():
@@ -180,7 +187,7 @@
 
     @pl.loop(1, n)
     def _(k):
-        heights(k).start()
+        heights(n - k).start()
 
     @pl.when(lat > 0)
     def _():
@@ -209,8 +216,8 @@
 
     @pl.loop(1, n)
     def _(k):
-        extras(k, ws)
-        weights(k).start()
+        extras(n - k, ws)
+        weights(n - k).start()
 
     extras(0, wr)
 
@@ -297,7 +304,7 @@
         D[8:top, cols] = (MU_DATA * field(0) + (RIDGE + 4.0 - SHIFT)) * inv
         return rolled
 
-    east_last = lax.fori_loop(0, blocks, assemble, jnp.zeros((rows, LANES), F32), unroll=2)
+    east_last = lax.fori_loop(0, blocks, assemble, jnp.zeros((rows, LANES), F32), unroll=8)
 
     first = slice(LANES, 2 * LANES)
     final = slice(blocks * LANES, (blocks + 1) * LANES)
@@ -413,7 +420,7 @@
         _, here, before, ahead = one(0, here, ahead, ahead)
         zero = jnp.zeros((8, LANES), F32)
         here, before, ahead, cross, own, base = lax.fori_loop(
-            1, blocks + 1, step, (here, before, ahead, zero, zero, zero), unroll=2
+            1, blocks + 1, step, (here, before, ahead, zero, zero, zero), unroll=8
         )
         if k < ITERS - 1:
             one(ext - 1, here, before, ahead)
@@ -523,7 +530,7 @@
             return carry
 
         per = width // LANES
-        lax.fori_loop(c * per, (c + 1) * per, one, 0, unroll=4)
+        lax.fori_loop(c * per, (c + 1) * per, one, 0, unroll=8)
         for copy in copies(c):
             copy.start()
     for c in range(CHUNKS):

time: 48.5 us -> 47.8 us (0.986)
  Pallas kernels: 47.7 us -> 47 us
    pallas_call x1, Pallas kernels: 46.6 us -> 45.9 us  [body(): pl.pallas_call(functools.partial(kernel, n, lats, pieces, rows), out_shap...]
where the time goes in v3:
time: 47.8 us; the launch traced here: 47.6 us
  Pallas kernels  47 us (98%)
  between operations  0.64 us (1%)
    pallas_call x1, Pallas kernels, body(): pl.pallas_call(functools.partial(kernel, n, lats, pieces, rows), out_shap...  45.9 us
    pallas_call x1, Pallas kernels, body(): pl.pallas_call(functools.partial(combine, rows), out_shape=(out, out), in...  1.07 us

profile of v3, /device:TPU:0, one launch (start us, length us, event | category | flops | bytes accessed | tf_op | source)
XLA Modules:
  0.0 47.6 jit_solution(13870013420010266316)
XLA Ops:
  0.6 45.9 %shard_map.59 = (f32[5,48,4352]{2,1,0:T(8,128)S(1)}, f32[16,128]{1,0:T(8,128)S(1)}) custom-call(s32[8]{0:T(128)} %col_in.1, s32[8]{0:T(128)} %wid_in.1, f32[8,32,128]{2,1,0:T(8,128)} %h_in.1, f32[8,32,128]{2,1,0:T(8,128)} %w_in.1), custom_call_target="tpu_custom_call" | custom-call | tf_op jit(solution)/shard_map/pallas_call | solution.py:590
  46.6 1.1 %shard_map.60 = (f32[32,4096]{1,0:T(8,128)}, f32[32,4096]{1,0:T(8,128)}) custom-call(f32[5,48,4352]{2,1,0:T(8,128)S(1)} %get-tuple-element.4.V, f32[16,128]{1,0:T(8,128)S(1)} %get-tuple-element.5.coef_ref), custom_call_target="tpu_custom_call" | custom-call | tf_op jit(solution)/shard_map/pallas_call | solution.py:604

commit v4 on v3

--- a/solution.py
+++ b/solution.py
@@ -76,6 +76,7 @@
     hs, ws, hr, wr, ms, mr, msm, idx_s, up_s, up_r, dn_s, dn_r,
     blk_s, prev_s, last_v, last_s, S,
     D, east_s, east_r, west_s, west_r, lat_up_s, lat_up_r, lat_dn_s, lat_dn_r,
+    side_up_s, side_up_r, side_dn_s, side_dn_r,
     red, ra, rb,
     sem_m, sem_h, sem_w, sem_e, sem_l, sem_t, sem_a, sem_b, sem_loc,
 ):
@@ -150,11 +151,11 @@
             w_to[k, q * rows : (q + 1) * rows, :] = jnp.where(lane < limit, w_ref[at], 0.0)
         m_to[k] = jnp.where(lane1 == 0, tags[0], jnp.where(lane1 == 1, tags[1], -1))
 
-    fill(0, hr, wr, mr)
-
-    @pl.loop(1, n)
-    def _(k):
-        fill(n - k, hs, ws, ms)
+    far = n // 2
+
+    @pl.loop(0, far)
+    def _(i):
+        fill(n - 1 - i, hs, ws, ms)
 
     pl.semaphore_wait(barrier, n - 1 + lats - 1)
 
@@ -181,13 +182,18 @@
     def _():
         edge_dn().start()
 
-    @pl.loop(1, n)
-    def _(k):
-        meta(k).start()
-
-    @pl.loop(1, n)
-    def _(k):
-        heights(n - k).start()
+    @pl.loop(0, far)
+    def _(i):
+        meta(n - 1 - i).start()
+        heights(n - 1 - i).start()
+
+    @pl.loop(far, n - 1)
+    def _(i):
+        fill(n - 1 - i, hs, ws, ms)
+        meta(n - 1 - i).start()
+        heights(n - 1 - i).start()
+
+    fill(0, hr, wr, mr)
 
     @pl.when(lat > 0)
     def _():
@@ -229,10 +235,13 @@
     tags_in.start()
     tags_in.wait()
 
-    @pl.loop(0, n)
-    def _(k):
-        blk_s[2 * k] = msm[k, 0, 0]
-        blk_s[2 * k + 1] = msm[k, 0, 1]
+    blk_s[0] = msm[0, 0, 0]
+    blk_s[1] = msm[0, 0, 1]
+
+    @pl.loop(1, n)
+    def _(i):
+        blk_s[2 * i] = msm[n - i, 0, 0]
+        blk_s[2 * i + 1] = msm[n - i, 0, 1]
 
     def latest(p, last):
         tag = blk_s[p]
@@ -253,9 +262,9 @@
     has_north = row_global < lats * rows - 1
     row_in = lax.broadcasted_iota(jnp.int32, (rows, LANES), 0)
 
-    def terms(k):
+    def terms(k, place):
         for q in range(2):
-            p = 2 * k + q
+            p = 2 * place + q
             before = prev_s[p]
             h = hr[k, q * rows : (q + 1) * rows, :]
             w = wr[k, q * rows : (q + 1) * rows, :]
@@ -275,13 +284,13 @@
             S[p, at : at + 1, :] = below_w + S[before, at : at + 1, :]
             S[p, at + 1 : at + 2, :] = below_w * (h[0:1, :] - below_h) + S[before, at + 1 : at + 2, :]
 
-    terms(0)
-
-    @pl.loop(1, n)
-    def _(k):
-        heights(k).wait_recv()
-        weights(k).wait_recv()
-        terms(k)
+    terms(0, 0)
+
+    @pl.loop(1, n)
+    def _(i):
+        heights(n - i).wait_recv()
+        weights(n - i).wait_recv()
+        terms(n - i, i)
 
     inv = 1.0 / SCALE
 
@@ -317,34 +326,57 @@
     west = remote(west_s, west_r, sem_l.at[2], sem_l.at[3], (lon_at(n - 1), lat))
     east.start()
     west.start()
-    east.wait_recv()
+
+    inner = slice(LANES, (blocks + 1) * LANES)
+    lat_up_s[0:4, :] = D[top - 4 : top, inner]
+    lat_up_s[4:8, :] = V[0, top - 4 : top, inner]
+    lat_dn_s[0:4, :] = V[0, 8:12, inner]
+    lat_dn_s[4:8, :] = D[8:12, inner]
+
+    def rows_up():
+        return remote(lat_up_s, lat_up_r, sem_t.at[0], sem_t.at[1], (lon, lat_at(1)))
+
+    def rows_dn():
+        return remote(lat_dn_s, lat_dn_r, sem_t.at[2], sem_t.at[3], (lon, lat_at(lats - 1)))
+
+    def sides_up():
+        return remote(side_up_s, side_up_r, sem_t.at[4], sem_t.at[5], (lon, lat_at(1)))
+
+    def sides_dn():
+        return remote(side_dn_s, side_dn_r, sem_t.at[6], sem_t.at[7], (lon, lat_at(lats - 1)))
+
+    @pl.when(lat < lats - 1)
+    def _():
+        rows_up().start()
+
+    @pl.when(lat > 0)
+    def _():
+        rows_dn().start()
+
     halo_w = slice(0, LANES)
     halo_e = slice((blocks + 1) * LANES, (blocks + 2) * LANES)
+    east.wait_recv()
     V[0, 8:top, halo_w] = east_r[0:rows, :]
     D[8:top, halo_w] = east_r[rows : 2 * rows, :]
     V[0, 8:top, first] = V[0, 8:top, first] + jnp.where(lane == 0, east_r[2 * rows : 3 * rows, :], 0.0)
     west.wait_recv()
     V[0, 8:top, halo_e] = west_r[0:rows, :] + jnp.where(lane == 0, east_last, 0.0)
     D[8:top, halo_e] = west_r[rows : 2 * rows, :]
-
-    lat_up_s[0:4, :] = D[top - 4 : top, :]
-    lat_up_s[4:8, :] = V[0, top - 4 : top, :]
-    lat_dn_s[0:4, :] = V[0, 8:12, :]
-    lat_dn_s[4:8, :] = D[8:12, :]
-
-    def rows_up():
-        return remote(lat_up_s, lat_up_r, sem_t.at[0], sem_t.at[1], (lon, lat_at(1)))
-
-    def rows_dn():
-        return remote(lat_dn_s, lat_dn_r, sem_t.at[2], sem_t.at[3], (lon, lat_at(lats - 1)))
+    side_blocks = (halo_w, first, halo_e)
+    for i, cols in enumerate(side_blocks):
+        to = slice(i * LANES, (i + 1) * LANES)
+        side_up_s[0:4, to] = D[top - 4 : top, cols]
+        side_up_s[4:8, to] = V[0, top - 4 : top, cols]
+        side_dn_s[0:4, to] = V[0, 8:12, cols]
+        side_dn_s[4:8, to] = D[8:12, cols]
 
     @pl.when(lat < lats - 1)
     def _():
-        rows_up().start()
+        sides_up().start()
 
     @pl.when(lat > 0)
     def _():
-        rows_dn().start()
+        sides_dn().start()
 
     def mirror(k):
         @pl.when(lat == 0)
@@ -359,8 +391,13 @@
     def _():
         rows_up().wait_recv()
         got = lat_up_r[...]
-        V[0, 0:8, :] = got
-        D[0:8, :] = pltpu.roll(got, 4, 0)
+        V[0, 0:8, inner] = got
+        D[0:8, inner] = pltpu.roll(got, 4, 0)
+        sides_up().wait_recv()
+        for i, cols in enumerate(side_blocks):
+            got = side_up_r[:, i * LANES : (i + 1) * LANES]
+            V[0, 0:8, cols] = got
+            D[0:8, cols] = pltpu.roll(got, 4, 0)
 
     @pl.when(lat == 0)
     def _():
@@ -371,8 +408,13 @@
     def _():
         rows_dn().wait_recv()
         got = lat_dn_r[...]
-        V[0, top : top + 8, :] = got
-        D[top : top + 8, :] = pltpu.roll(got, 4, 0)
+        V[0, top : top + 8, inner] = got
+        D[top : top + 8, inner] = pltpu.roll(got, 4, 0)
+        sides_dn().wait_recv()
+        for i, cols in enumerate(side_blocks):
+            got = side_dn_r[:, i * LANES : (i + 1) * LANES]
+            V[0, top : top + 8, cols] = got
+            D[top : top + 8, cols] = pltpu.roll(got, 4, 0)
 
     @pl.when(lat == lats - 1)
     def _():
@@ -494,11 +536,13 @@
     def _():
         edge_up().wait_send()
         rows_up().wait_send()
+        sides_up().wait_send()
 
     @pl.when(lat > 0)
     def _():
         edge_dn().wait_send()
         rows_dn().wait_send()
+        sides_dn().wait_send()
 
 
 def combine(rows, V, coef_ref, x_out, r_out, x_ref, r_ref, sem):
@@ -570,10 +614,14 @@
         vmem((3 * rows, LANES), F32),
         vmem((2 * rows, LANES), F32),
         vmem((2 * rows, LANES), F32),
-        vmem((8, ext), F32),
-        vmem((8, ext), F32),
-        vmem((8, ext), F32),
-        vmem((8, ext), F32),
+        vmem((8, COLS_DEV), F32),
+        vmem((8, COLS_DEV), F32),
+        vmem((8, COLS_DEV), F32),
+        vmem((8, COLS_DEV), F32),
+        vmem((8, 3 * LANES), F32),
+        vmem((8, 3 * LANES), F32),
+        vmem((8, 3 * LANES), F32),
+        vmem((8, 3 * LANES), F32),
         vmem((16, LANES), F32),
         vmem((lats, 16, LANES), F32),
         vmem((n, 16, LANES), F32),
@@ -582,7 +630,7 @@
         dma((2, n)),
         dma((4,)),
         dma((4,)),
-        dma((4,)),
+        dma((8,)),
         dma((2, lats)),
         dma((2, n)),
         dma((6,)),

time: 47.8 us -> 46.5 us (0.973)
  Pallas kernels: 47 us -> 45.7 us
    pallas_call x1, Pallas kernels: 45.9 us -> 44.7 us  [body(): pl.pallas_call(functools.partial(kernel, n, lats, pieces, rows), out_shap...]
where the time goes in v4:
time: 46.5 us; the launch traced here: 46.4 us
  Pallas kernels  45.7 us (98%)
  between operations  0.64 us (1%)
    pallas_call x1, Pallas kernels, body(): pl.pallas_call(functools.partial(kernel, n, lats, pieces, rows), out_shap...  44.7 us
    pallas_call x1, Pallas kernels, body(): pl.pallas_call(functools.partial(combine, rows), out_shape=(out, out), in...  1.07 us

profile of v4, /device:TPU:0, one launch (start us, length us, event | category | flops | bytes accessed | tf_op | source)
XLA Modules:
  0.0 46.4 jit_solution(15203135420196509545)
XLA Ops:
  0.6 44.7 %shard_map.59 = (f32[5,48,4352]{2,1,0:T(8,128)S(1)}, f32[16,128]{1,0:T(8,128)S(1)}) custom-call(s32[8]{0:T(128)} %col_in.1, s32[8]{0:T(128)} %wid_in.1, f32[8,32,128]{2,1,0:T(8,128)} %h_in.1, f32[8,32,128]{2,1,0:T(8,128)} %w_in.1), custom_call_target="tpu_custom_call" | custom-call | tf_op jit(solution)/shard_map/pallas_call | solution.py:638
  45.3 1.1 %shard_map.60 = (f32[32,4096]{1,0:T(8,128)}, f32[32,4096]{1,0:T(8,128)}) custom-call(f32[5,48,4352]{2,1,0:T(8,128)S(1)} %get-tuple-element.4.V, f32[16,128]{1,0:T(8,128)S(1)} %get-tuple-element.5.coef_ref), custom_call_target="tpu_custom_call" | custom-call | tf_op jit(solution)/shard_map/pallas_call | solution.py:652

commit v5 on v4

--- a/solution.py
+++ b/solution.py
@@ -77,8 +77,8 @@
     blk_s, prev_s, last_v, last_s, S,
     D, east_s, east_r, west_s, west_r, lat_up_s, lat_up_r, lat_dn_s, lat_dn_r,
     side_up_s, side_up_r, side_dn_s, side_dn_r,
-    red, ra, rb,
-    sem_m, sem_h, sem_w, sem_e, sem_l, sem_t, sem_a, sem_b, sem_loc,
+    red, rb,
+    sem_m, sem_h, sem_w, sem_e, sem_l, sem_t, sem_b, sem_loc,
 ):
     lon = lax.axis_index("lon")
     lat = lax.axis_index("lat")
@@ -112,13 +112,14 @@
     for load in loads:
         load.start()
 
-    @pl.loop(1, n)
-    def _(k):
-        pl.semaphore_signal(barrier, inc=1, device_id=(partner(k), lat), device_id_type=MESH)
-
-    @pl.loop(1, lats)
-    def _(k):
-        pl.semaphore_signal(barrier, inc=1, device_id=(lon, lat_at(k)), device_id_type=MESH)
+    devices = n * lats
+
+    def peer(j):
+        return partner(j // lats), lat_at(j % lats)
+
+    @pl.loop(1, devices)
+    def _(j):
+        pl.semaphore_signal(barrier, inc=1, device_id=peer(j), device_id_type=MESH)
 
     for load in loads:
         load.wait()
@@ -157,7 +158,7 @@
     def _(i):
         fill(n - 1 - i, hs, ws, ms)
 
-    pl.semaphore_wait(barrier, n - 1 + lats - 1)
+    pl.semaphore_wait(barrier, devices - 1)
 
     def edge_up():
         return remote(up_s, up_r, sem_e.at[0], sem_e.at[1], (lon, lat_at(1)))
@@ -317,11 +318,16 @@
 
     first = slice(LANES, 2 * LANES)
     final = slice(blocks * LANES, (blocks + 1) * LANES)
-    east_s[0:rows, :] = V[0, 8:top, final]
-    east_s[rows : 2 * rows, :] = D[8:top, final]
-    east_s[2 * rows : 3 * rows, :] = east_last
-    west_s[0:rows, :] = V[0, 8:top, first]
-    west_s[rows : 2 * rows, :] = D[8:top, first]
+    east_s[...] = jnp.where(
+        lane >= LANES - 4,
+        V[0, 8:top, final],
+        jnp.where(
+            lane >= LANES - 8,
+            pltpu.roll(D[8:top, final], LANES - 4, 1),
+            pltpu.roll(east_last, LANES - 9, 1),
+        ),
+    )
+    west_s[...] = jnp.where(lane < 4, V[0, 8:top, first], pltpu.roll(D[8:top, first], 4, 1))
     east = remote(east_s, east_r, sem_l.at[0], sem_l.at[1], (lon_at(1), lat))
     west = remote(west_s, west_r, sem_l.at[2], sem_l.at[3], (lon_at(n - 1), lat))
     east.start()
@@ -356,12 +362,14 @@
     halo_w = slice(0, LANES)
     halo_e = slice((blocks + 1) * LANES, (blocks + 2) * LANES)
     east.wait_recv()
-    V[0, 8:top, halo_w] = east_r[0:rows, :]
-    D[8:top, halo_w] = east_r[rows : 2 * rows, :]
-    V[0, 8:top, first] = V[0, 8:top, first] + jnp.where(lane == 0, east_r[2 * rows : 3 * rows, :], 0.0)
+    got_east = east_r[...]
+    V[0, 8:top, halo_w] = got_east
+    D[8:top, halo_w] = pltpu.roll(got_east, 4, 1)
+    V[0, 8:top, first] = V[0, 8:top, first] + jnp.where(lane == 0, pltpu.roll(got_east, 9, 1), 0.0)
     west.wait_recv()
-    V[0, 8:top, halo_e] = west_r[0:rows, :] + jnp.where(lane == 0, east_last, 0.0)
-    D[8:top, halo_e] = west_r[rows : 2 * rows, :]
+    got_west = west_r[...]
+    V[0, 8:top, halo_e] = got_west + jnp.where(lane == 0, east_last, 0.0)
+    D[8:top, halo_e] = pltpu.roll(got_west, LANES - 4, 1)
     side_blocks = (halo_w, first, halo_e)
     for i, cols in enumerate(side_blocks):
         to = slice(i * LANES, (i + 1) * LANES)
@@ -476,47 +484,31 @@
             sums.append(base)
         sums += [cross, own]
 
-    red[...] = jnp.zeros_like(red)
+    mine = jnp.zeros((1, LANES), F32)
     for i, value in enumerate(sums):
-        red[i : i + 1, :] = jnp.sum(value, axis=0, keepdims=True)
-
-    def over_lat(k):
-        return remote(red, ra.at[lat], sem_a.at[0, k], sem_a.at[1, k], (lon, lat_at(k)))
-
-    def over_lon(k):
-        return remote(red, rb.at[lon], sem_b.at[0, k], sem_b.at[1, k], (lon_at(k), lat))
-
-    @pl.loop(1, lats)
-    def _(k):
-        over_lat(k).start()
-
-    ra[lat] = red[...]
-
-    @pl.loop(1, lats)
-    def _(k):
-        over_lat(k).wait()
-
-    total = ra[0]
-    for i in range(1, lats):
-        total = total + ra[i]
-    red[...] = total
-
-    @pl.loop(1, n)
-    def _(k):
-        over_lon(k).start()
-
-    rb[lon] = red[...]
-
-    @pl.loop(1, n)
-    def _(k):
-        over_lon(k).wait()
-
-    total = rb[0]
-    for i in range(1, n):
-        total = total + rb[i]
-
+        value = jnp.sum(jnp.sum(value, axis=0, keepdims=True), axis=1, keepdims=True)
+        mine = jnp.where(lane1 == i, value, mine)
+    red[...] = mine
+    place = lon * lats + lat
+
+    def share(j):
+        return remote(red, rb.at[place], sem_b.at[0, j], sem_b.at[1, j], peer(j))
+
+    @pl.loop(1, devices)
+    def _(j):
+        share(devices - j).start()
+
+    rb[place] = mine
+
+    @pl.loop(1, devices)
+    def _(j):
+        share(j).wait_recv()
+
+    total = jnp.sum(rb[...], axis=0)
     mu = [
-        jnp.broadcast_to(jnp.sum(total[i : i + 1, :], axis=1, keepdims=True), (8, LANES))
+        jnp.broadcast_to(
+            jnp.sum(jnp.where(lane1 == i, total, 0.0), axis=1, keepdims=True), (8, LANES)
+        )
         for i in range(2 * ITERS + 1)
     ]
     field, residual = cg_coefficients(mu)
@@ -528,6 +520,10 @@
         meta(k).wait_send()
         heights(k).wait_send()
         weights(k).wait_send()
+
+    @pl.loop(1, devices)
+    def _(j):
+        share(j).wait_send()
 
     east.wait_send()
     west.wait_send()
@@ -610,10 +606,10 @@
         pltpu.SMEM((1, LANES), jnp.int32),
         vmem((2 * n + 1, 6 * rows + 8, LANES), F32),
         vmem((rows + 16, ext), F32),
-        vmem((3 * rows, LANES), F32),
-        vmem((3 * rows, LANES), F32),
-        vmem((2 * rows, LANES), F32),
-        vmem((2 * rows, LANES), F32),
+        vmem((rows, LANES), F32),
+        vmem((rows, LANES), F32),
+        vmem((rows, LANES), F32),
+        vmem((rows, LANES), F32),
         vmem((8, COLS_DEV), F32),
         vmem((8, COLS_DEV), F32),
         vmem((8, COLS_DEV), F32),
@@ -622,17 +618,15 @@
         vmem((8, 3 * LANES), F32),
         vmem((8, 3 * LANES), F32),
         vmem((8, 3 * LANES), F32),
-        vmem((16, LANES), F32),
-        vmem((lats, 16, LANES), F32),
-        vmem((n, 16, LANES), F32),
+        vmem((1, LANES), F32),
+        vmem((n * lats, 1, LANES), F32),
         dma((2, n)),
         dma((2, n)),
         dma((2, n)),
         dma((4,)),
         dma((4,)),
         dma((8,)),
-        dma((2, lats)),
-        dma((2, n)),
+        dma((2, n * lats)),
         dma((6,)),
     ]
     basis, coef = pl.pallas_call(

time: 46.5 us -> 46.6 us (level)
  no operation moved by 1% of the time
where the time goes in v5:
time: 46.6 us; the launch traced here: 46.5 us
  Pallas kernels  45.8 us (98%)
  between operations  0.64 us (1%)
    pallas_call x1, Pallas kernels, body(): pl.pallas_call(functools.partial(kernel, n, lats, pieces, rows), out_shap...  44.8 us
    pallas_call x1, Pallas kernels, body(): pl.pallas_call(functools.partial(combine, rows), out_shape=(out, out), in...  1.07 us

profile of v5, /device:TPU:0, one launch (start us, length us, event | category | flops | bytes accessed | tf_op | source)
XLA Modules:
  0.0 46.5 jit_solution(2546332338519379009)
XLA Ops:
  0.6 44.8 %shard_map.59 = (f32[5,48,4352]{2,1,0:T(8,128)S(1)}, f32[16,128]{1,0:T(8,128)S(1)}) custom-call(s32[8]{0:T(128)} %col_in.1, s32[8]{0:T(128)} %wid_in.1, f32[8,32,128]{2,1,0:T(8,128)} %h_in.1, f32[8,32,128]{2,1,0:T(8,128)} %w_in.1), custom_call_target="tpu_custom_call" | custom-call | tf_op jit(solution)/shard_map/pallas_call | solution.py:632
  45.4 1.1 %shard_map.60 = (f32[32,4096]{1,0:T(8,128)}, f32[32,4096]{1,0:T(8,128)}) custom-call(f32[5,48,4352]{2,1,0:T(8,128)S(1)} %get-tuple-element.4.V, f32[16,128]{1,0:T(8,128)S(1)} %get-tuple-element.5.coef_ref), custom_call_target="tpu_custom_call" | custom-call | tf_op jit(solution)/shard_map/pallas_call | solution.py:646

commit v6 on v5

--- a/solution.py
+++ b/solution.py
@@ -26,6 +26,17 @@
         src_ref=src, dst_ref=dst, send_sem=send, recv_sem=recv,
         device_id=device, device_id_type=MESH,
     )
+
+
+def each(low, high):
+    def run(step):
+        if high - low <= 32:
+            for i in range(low, high):
+                step(i)
+        else:
+            pl.loop(low, high)(step)
+
+    return run
 
 
 def cg_coefficients(mu):
@@ -92,15 +103,25 @@
     def lon_at(k):
         return lax.rem(lon + k, n)
 
+    turns, bit = [], 1
+    while bit < n:
+        turns.append((1 - 2 * (lon // bit % 2)) * bit)
+        bit *= 2
+
     def partner(k):
-        other, bit = jnp.int32(0), 1
-        while bit < n:
-            other = other + (lon // bit + k // bit) % 2 * bit
-            bit *= 2
+        other = lon
+        for i, turn in enumerate(turns):
+            if isinstance(k, int):
+                other = other + turn if k >> i & 1 else other
+            else:
+                other = other + k // 2**i % 2 * turn
         return other
 
     def lat_at(k):
-        return lax.rem(lat + k, lats)
+        if isinstance(k, int) and k == 0:
+            return lat
+        moved = lat + k
+        return jnp.where(moved >= lats, moved - lats, moved)
 
     barrier = pltpu.get_barrier_semaphore()
     loads = [
@@ -117,7 +138,7 @@
     def peer(j):
         return partner(j // lats), lat_at(j % lats)
 
-    @pl.loop(1, devices)
+    @each(1, devices)
     def _(j):
         pl.semaphore_signal(barrier, inc=1, device_id=peer(j), device_id_type=MESH)
 
@@ -154,7 +175,7 @@
 
     far = n // 2
 
-    @pl.loop(0, far)
+    @each(0, far)
     def _(i):
         fill(n - 1 - i, hs, ws, ms)
 
@@ -183,12 +204,12 @@
     def _():
         edge_dn().start()
 
-    @pl.loop(0, far)
+    @each(0, far)
     def _(i):
         meta(n - 1 - i).start()
         heights(n - 1 - i).start()
 
-    @pl.loop(far, n - 1)
+    @each(far, n - 1)
     def _(i):
         fill(n - 1 - i, hs, ws, ms)
         meta(n - 1 - i).start()
@@ -221,14 +242,14 @@
             w_to[k, base + 4 : base + 5, :] = jnp.where(lane1 < limit, up_r[1, pl.ds(at, 1), :], 0.0)
         w_to[k, 2 * rows + 6 : 2 * rows + 8, :] = jnp.zeros((2, LANES), F32)
 
-    @pl.loop(1, n)
+    @each(1, n)
     def _(k):
         extras(n - k, ws)
         weights(n - k).start()
 
     extras(0, wr)
 
-    @pl.loop(1, n)
+    @each(1, n)
     def _(k):
         meta(k).wait_recv()
 
@@ -239,7 +260,7 @@
     blk_s[0] = msm[0, 0, 0]
     blk_s[1] = msm[0, 0, 1]
 
-    @pl.loop(1, n)
+    @each(1, n)
     def _(i):
         blk_s[2 * i] = msm[n - i, 0, 0]
         blk_s[2 * i + 1] = msm[n - i, 0, 1]
@@ -253,7 +274,18 @@
         prev_s[p] = lax.fori_loop(0, slots, scan, jnp.int32(slots), unroll=8)
         return jnp.where(lane1 == tag, p, last)
 
-    last_v[...] = lax.fori_loop(0, slots, latest, jnp.full((1, LANES), slots, jnp.int32))
+    nowhere = jnp.full((1, LANES), slots, jnp.int32)
+    if slots <= 16:
+        tags = [blk_s[p] for p in range(slots)]
+        for p, tag in enumerate(tags):
+            found = jnp.int32(slots)
+            for j in range(p):
+                found = jnp.where(tags[j] == tag, j, found)
+            prev_s[p] = found
+            nowhere = jnp.where(lane1 == tag, p, nowhere)
+        last_v[...] = nowhere
+    else:
+        last_v[...] = lax.fori_loop(0, slots, latest, nowhere)
     last_in = pltpu.make_async_copy(last_v, last_s, sem_loc.at[1])
     last_in.start()
     last_in.wait()
@@ -287,7 +319,7 @@
 
     terms(0, 0)
 
-    @pl.loop(1, n)
+    @each(1, n)
     def _(i):
         heights(n - i).wait_recv()
         weights(n - i).wait_recv()
@@ -494,13 +526,13 @@
     def share(j):
         return remote(red, rb.at[place], sem_b.at[0, j], sem_b.at[1, j], peer(j))
 
-    @pl.loop(1, devices)
+    @each(1, devices)
     def _(j):
         share(devices - j).start()
 
     rb[place] = mine
 
-    @pl.loop(1, devices)
+    @each(1, devices)
     def _(j):
         share(j).wait_recv()
 
@@ -515,13 +547,13 @@
     for i, c in enumerate(field + residual):
         coef_ref[i : i + 1, :] = c[0:1, :]
 
-    @pl.loop(1, n)
+    @each(1, n)
     def _(k):
         meta(k).wait_send()
         heights(k).wait_send()
         weights(k).wait_send()
 
-    @pl.loop(1, devices)
+    @each(1, devices)
     def _(j):
         share(j).wait_send()
 

time: 46.6 us -> 46.2 us (level)
  no operation moved by 1% of the time
where the time goes in v6:
time: 46.2 us; the launch traced here: 46.1 us
  Pallas kernels  45.4 us (98%)
  between operations  0.64 us (1%)
    pallas_call x1, Pallas kernels, body(): pl.pallas_call(functools.partial(kernel, n, lats, pieces, rows), out_shap...  44.3 us
    pallas_call x1, Pallas kernels, body(): pl.pallas_call(functools.partial(combine, rows), out_shape=(out, out), in...  1.07 us

profile of v6, /device:TPU:0, one launch (start us, length us, event | category | flops | bytes accessed | tf_op | source)
XLA Modules:
  0.0 46.1 jit_solution(7226015608459477176)
XLA Ops:
  0.6 44.3 %shard_map.59 = (f32[5,48,4352]{2,1,0:T(8,128)S(1)}, f32[16,128]{1,0:T(8,128)S(1)}) custom-call(s32[8]{0:T(128)} %col_in.1, s32[8]{0:T(128)} %wid_in.1, f32[8,32,128]{2,1,0:T(8,128)} %h_in.1, f32[8,32,128]{2,1,0:T(8,128)} %w_in.1), custom_call_target="tpu_custom_call" | custom-call | tf_op jit(solution)/shard_map/pallas_call | solution.py:664
  45.0 1.1 %shard_map.60 = (f32[32,4096]{1,0:T(8,128)}, f32[32,4096]{1,0:T(8,128)}) custom-call(f32[5,48,4352]{2,1,0:T(8,128)S(1)} %get-tuple-element.4.V, f32[16,128]{1,0:T(8,128)S(1)} %get-tuple-element.5.coef_ref), custom_call_target="tpu_custom_call" | custom-call | tf_op jit(solution)/shard_map/pallas_call | solution.py:678

commit v7 on v6

--- a/solution.py
+++ b/solution.py
@@ -30,7 +30,7 @@
 
 def each(low, high):
     def run(step):
-        if high - low <= 32:
+        if high - low <= 8:
             for i in range(low, high):
                 step(i)
         else:
@@ -88,7 +88,7 @@
     blk_s, prev_s, last_v, last_s, S,
     D, east_s, east_r, west_s, west_r, lat_up_s, lat_up_r, lat_dn_s, lat_dn_r,
     side_up_s, side_up_r, side_dn_s, side_dn_r,
-    red, rb,
+    red, rb, acc,
     sem_m, sem_h, sem_w, sem_e, sem_l, sem_t, sem_b, sem_loc,
 ):
     lon = lax.axis_index("lon")
@@ -135,12 +135,16 @@
 
     devices = n * lats
 
-    def peer(j):
-        return partner(j // lats), lat_at(j % lats)
-
-    @each(1, devices)
-    def _(j):
-        pl.semaphore_signal(barrier, inc=1, device_id=peer(j), device_id_type=MESH)
+    def all_peers(step):
+        each(1, n)(lambda k: step(k * lats, (partner(k), lat)))
+
+        @pl.loop(1, lats)
+        def _(m):
+            each(0, n)(lambda k: step(k * lats + m, (partner(k), lat_at(m))))
+
+    all_peers(
+        lambda j, device: pl.semaphore_signal(barrier, inc=1, device_id=device, device_id_type=MESH)
+    )
 
     for load in loads:
         load.wait()
@@ -346,7 +350,7 @@
         D[8:top, cols] = (MU_DATA * field(0) + (RIDGE + 4.0 - SHIFT)) * inv
         return rolled
 
-    east_last = lax.fori_loop(0, blocks, assemble, jnp.zeros((rows, LANES), F32), unroll=8)
+    east_last = lax.fori_loop(0, blocks, assemble, jnp.zeros((rows, LANES), F32), unroll=4)
 
     first = slice(LANES, 2 * LANES)
     final = slice(blocks * LANES, (blocks + 1) * LANES)
@@ -475,7 +479,8 @@
             total = total + value[8 * i : 8 * i + 8]
         return total
 
-    def apply(k):
+    @pl.loop(0, ITERS)
+    def _(k):
         def one(b, here, before, ahead):
             nxt = V[k, :, at_block(jnp.minimum(b + 1, ext - 1))]
             ahead_next = pltpu.roll(nxt, LANES - 1, 1)
@@ -488,47 +493,38 @@
             return out, nxt, rolled, ahead_next
 
         def step(b, carry):
-            here, before, ahead, cross, own, base = carry
+            here, before, ahead, base, cross, own = carry
             out, nxt, rolled, ahead_next = one(b, here, before, ahead)
             mine, image = here[8:top], out[8:top]
+            base = base + fold(mine * mine)
             cross = cross + fold(mine * image)
             own = own + fold(image * image)
-            if k == 0:
-                base = base + fold(mine * mine)
-            return nxt, rolled, ahead_next, cross, own, base
+            return nxt, rolled, ahead_next, base, cross, own
 
         here = V[k, :, 0:LANES]
         ahead = pltpu.roll(here, LANES - 1, 1)
         _, here, before, ahead = one(0, here, ahead, ahead)
         zero = jnp.zeros((8, LANES), F32)
-        here, before, ahead, cross, own, base = lax.fori_loop(
-            1, blocks + 1, step, (here, before, ahead, zero, zero, zero), unroll=8
+        here, before, ahead, base, cross, own = lax.fori_loop(
+            1, blocks + 1, step, (here, before, ahead, zero, zero, zero), unroll=4
         )
-        if k < ITERS - 1:
-            one(ext - 1, here, before, ahead)
-            mirror(k + 1)
-        return cross, own, base
-
-    sums = []
-    for k in range(ITERS):
-        cross, own, base = apply(k)
-        if k == 0:
-            sums.append(base)
-        sums += [cross, own]
+        one(ext - 1, here, before, ahead)
+        mirror(k + 1)
+        acc[2 * k] = base
+        acc[2 * k + 1] = cross
+        acc[2 * k + 2] = own
 
     mine = jnp.zeros((1, LANES), F32)
-    for i, value in enumerate(sums):
-        value = jnp.sum(jnp.sum(value, axis=0, keepdims=True), axis=1, keepdims=True)
+    for i in range(2 * ITERS + 1):
+        value = jnp.sum(jnp.sum(acc[i], axis=0, keepdims=True), axis=1, keepdims=True)
         mine = jnp.where(lane1 == i, value, mine)
     red[...] = mine
     place = lon * lats + lat
 
-    def share(j):
-        return remote(red, rb.at[place], sem_b.at[0, j], sem_b.at[1, j], peer(j))
-
-    @each(1, devices)
-    def _(j):
-        share(devices - j).start()
+    def share(j, device=(partner(1), lat)):
+        return remote(red, rb.at[place], sem_b.at[0, j], sem_b.at[1, j], device)
+
+    all_peers(lambda j, device: share(j, device).start())
 
     rb[place] = mine
 
@@ -602,7 +598,7 @@
             return carry
 
         per = width // LANES
-        lax.fori_loop(c * per, (c + 1) * per, one, 0, unroll=8)
+        lax.fori_loop(c * per, (c + 1) * per, one, 0, unroll=4)
         for copy in copies(c):
             copy.start()
     for c in range(CHUNKS):
@@ -652,6 +648,7 @@
         vmem((8, 3 * LANES), F32),
         vmem((1, LANES), F32),
         vmem((n * lats, 1, LANES), F32),
+        vmem((2 * ITERS + 1, 8, LANES), F32),
         dma((2, n)),
         dma((2, n)),
         dma((2, n)),

time: 46.2 us -> 47.2 us (1.022)
  Pallas kernels: 45.4 us -> 46.4 us
    pallas_call x1, Pallas kernels: 44.3 us -> 45.3 us  [body(): pl.pallas_call(functools.partial(kernel, n, lats, pieces, rows), out_shap...]
where the time goes in v7:
time: 47.2 us; the launch traced here: 47.1 us
  Pallas kernels  46.4 us (98%)
  between operations  0.64 us (1%)
    pallas_call x1, Pallas kernels, body(): pl.pallas_call(functools.partial(kernel, n, lats, pieces, rows), out_shap...  45.3 us
    pallas_call x1, Pallas kernels, body(): pl.pallas_call(functools.partial(combine, rows), out_shape=(out, out), in...  1.1 us

profile of v7, /device:TPU:0, one launch (start us, length us, event | category | flops | bytes accessed | tf_op | source)
XLA Modules:
  0.0 47.1 jit_solution(15411436373418558849)
XLA Ops:
  0.6 45.3 %shard_map.59 = (f32[5,48,4352]{2,1,0:T(8,128)S(1)}, f32[16,128]{1,0:T(8,128)S(1)}) custom-call(s32[8]{0:T(128)} %col_in.1, s32[8]{0:T(128)} %wid_in.1, f32[8,32,128]{2,1,0:T(8,128)} %h_in.1, f32[8,32,128]{2,1,0:T(8,128)} %w_in.1), custom_call_target="tpu_custom_call" | custom-call | tf_op jit(solution)/shard_map/pallas_call | solution.py:661
  46.0 1.1 %shard_map.60 = (f32[32,4096]{1,0:T(8,128)}, f32[32,4096]{1,0:T(8,128)}) custom-call(f32[5,48,4352]{2,1,0:T(8,128)S(1)} %get-tuple-element.4.V, f32[16,128]{1,0:T(8,128)S(1)} %get-tuple-element.5.coef_ref), custom_call_target="tpu_custom_call" | custom-call | tf_op jit(solution)/shard_map/pallas_call | solution.py:675

commit v8 on v7

--- a/solution.py
+++ b/solution.py
@@ -350,7 +350,7 @@
         D[8:top, cols] = (MU_DATA * field(0) + (RIDGE + 4.0 - SHIFT)) * inv
         return rolled
 
-    east_last = lax.fori_loop(0, blocks, assemble, jnp.zeros((rows, LANES), F32), unroll=4)
+    east_last = lax.fori_loop(0, blocks, assemble, jnp.zeros((rows, LANES), F32), unroll=16)
 
     first = slice(LANES, 2 * LANES)
     final = slice(blocks * LANES, (blocks + 1) * LANES)
@@ -506,7 +506,7 @@
         _, here, before, ahead = one(0, here, ahead, ahead)
         zero = jnp.zeros((8, LANES), F32)
         here, before, ahead, base, cross, own = lax.fori_loop(
-            1, blocks + 1, step, (here, before, ahead, zero, zero, zero), unroll=4
+            1, blocks + 1, step, (here, before, ahead, zero, zero, zero), unroll=32
         )
         one(ext - 1, here, before, ahead)
         mirror(k + 1)
@@ -598,7 +598,7 @@
             return carry
 
         per = width // LANES
-        lax.fori_loop(c * per, (c + 1) * per, one, 0, unroll=4)
+        lax.fori_loop(c * per, (c + 1) * per, one, 0, unroll=8)
         for copy in copies(c):
             copy.start()
     for c in range(CHUNKS):

time: 47.2 us -> 37.3 us (0.79)
  Pallas kernels: 46.4 us -> 36.6 us
    pallas_call x1, Pallas kernels: 45.3 us -> 35.5 us  [body(): pl.pallas_call(functools.partial(kernel, n, lats, pieces, rows), out_shap...]
where the time goes in v8:
time: 37.3 us; the launch traced here: 37.2 us
  Pallas kernels  36.6 us (98%)
  between operations  0.64 us (2%)
    pallas_call x1, Pallas kernels, body(): pl.pallas_call(functools.partial(kernel, n, lats, pieces, rows), out_shap...  35.5 us
    pallas_call x1, Pallas kernels, body(): pl.pallas_call(functools.partial(combine, rows), out_shape=(out, out), in...  1.07 us

profile of v8, /device:TPU:0, one launch (start us, length us, event | category | flops | bytes accessed | tf_op | source)
XLA Modules:
  0.0 37.2 jit_solution(18387039042156322955)
XLA Ops:
  0.6 35.5 %shard_map.59 = (f32[5,48,4352]{2,1,0:T(8,128)S(1)}, f32[16,128]{1,0:T(8,128)S(1)}) custom-call(s32[8]{0:T(128)} %col_in.1, s32[8]{0:T(128)} %wid_in.1, f32[8,32,128]{2,1,0:T(8,128)} %h_in.1, f32[8,32,128]{2,1,0:T(8,128)} %w_in.1), custom_call_target="tpu_custom_call" | custom-call | tf_op jit(solution)/shard_map/pallas_call | solution.py:661
  36.1 1.1 %shard_map.60 = (f32[32,4096]{1,0:T(8,128)}, f32[32,4096]{1,0:T(8,128)}) custom-call(f32[5,48,4352]{2,1,0:T(8,128)S(1)} %get-tuple-element.4.V, f32[16,128]{1,0:T(8,128)S(1)} %get-tuple-element.5.coef_ref), custom_call_target="tpu_custom_call" | custom-call | tf_op jit(solution)/shard_map/pallas_call | solution.py:675

commit v9 on v8

--- a/solution.py
+++ b/solution.py
@@ -303,6 +303,9 @@
         for q in range(2):
             p = 2 * place + q
             before = prev_s[p]
+            so_far = [S[before, t * rows : (t + 1) * rows, :] for t in range(6)]
+            below_w_sum = S[before, 6 * rows : 6 * rows + 1, :]
+            below_sum = S[before, 6 * rows + 1 : 6 * rows + 2, :]
             h = hr[k, q * rows : (q + 1) * rows, :]
             w = wr[k, q * rows : (q + 1) * rows, :]
             base = 2 * rows + q
@@ -316,10 +319,10 @@
             parts = (w, w * h, w_east, w_east * (h_east - h), w_north, w_north * (h_north - h))
             for t, part in enumerate(parts):
                 at = pl.ds(t * rows, rows)
-                S[p, at, :] = part + S[before, at, :]
+                S[p, at, :] = part + so_far[t]
             at = 6 * rows
-            S[p, at : at + 1, :] = below_w + S[before, at : at + 1, :]
-            S[p, at + 1 : at + 2, :] = below_w * (h[0:1, :] - below_h) + S[before, at + 1 : at + 2, :]
+            S[p, at : at + 1, :] = below_w + below_w_sum
+            S[p, at + 1 : at + 2, :] = below_w * (h[0:1, :] - below_h) + below_sum
 
     terms(0, 0)
 
@@ -350,7 +353,7 @@
         D[8:top, cols] = (MU_DATA * field(0) + (RIDGE + 4.0 - SHIFT)) * inv
         return rolled
 
-    east_last = lax.fori_loop(0, blocks, assemble, jnp.zeros((rows, LANES), F32), unroll=16)
+    east_last = lax.fori_loop(0, blocks, assemble, jnp.zeros((rows, LANES), F32), unroll=32)
 
     first = slice(LANES, 2 * LANES)
     final = slice(blocks * LANES, (blocks + 1) * LANES)

time: 37.3 us -> 37.2 us (level)
  no operation moved by 1% of the time
where the time goes in v9:
time: 37.2 us; the launch traced here: 37 us
  Pallas kernels  36.4 us (98%)
  between operations  0.64 us (2%)
    pallas_call x1, Pallas kernels, body(): pl.pallas_call(functools.partial(kernel, n, lats, pieces, rows), out_shap...  35.3 us
    pallas_call x1, Pallas kernels, body(): pl.pallas_call(functools.partial(combine, rows), out_shape=(out, out), in...  1.07 us

profile of v9, /device:TPU:0, one launch (start us, length us, event | category | flops | bytes accessed | tf_op | source)
XLA Modules:
  0.0 37.0 jit_solution(15381645431646787005)
XLA Ops:
  0.6 35.3 %shard_map.59 = (f32[5,48,4352]{2,1,0:T(8,128)S(1)}, f32[16,128]{1,0:T(8,128)S(1)}) custom-call(s32[8]{0:T(128)} %col_in.1, s32[8]{0:T(128)} %wid_in.1, f32[8,32,128]{2,1,0:T(8,128)} %h_in.1, f32[8,32,128]{2,1,0:T(8,128)} %w_in.1), custom_call_target="tpu_custom_call" | custom-call | tf_op jit(solution)/shard_map/pallas_call | solution.py:664
  35.9 1.1 %shard_map.60 = (f32[32,4096]{1,0:T(8,128)}, f32[32,4096]{1,0:T(8,128)}) custom-call(f32[5,48,4352]{2,1,0:T(8,128)S(1)} %get-tuple-element.4.V, f32[16,128]{1,0:T(8,128)S(1)} %get-tuple-element.5.coef_ref), custom_call_target="tpu_custom_call" | custom-call | tf_op jit(solution)/shard_map/pallas_call | solution.py:678
